TPU v7x, 128 devices: a whole 4x4x4 slice. The times are simulated.
128 devices in a mesh: dp: 16 (over z_lo, y, core), tensor: 8 (over x, z_hi).
Axes of the slice: x: 4, y: 4, z: 4 (z_hi: 2, z_lo: 2; z = z_hi * 2 + z_lo), core: 2. Of those that a mesh axis runs over, the one named last changes fastest.
Arguments:
- attn_heads: bfloat16 [16384, 4096], P('dp', 'tensor'), may hold values from -3 to 3
- out_weight: bfloat16 [4096, 4096], P('tensor'), may hold values from -0.09375 to 0.09375
- residual: bfloat16 [16384, 4096], P(('dp', 'tensor')), may hold values from -6 to 6
- norm_gain: float32 [4096], replicated, may hold values from 0.1 to 1.9
- expert_ids: int32 [16384, 8], P(('dp', 'tensor')), may hold values from 0 to 127, all different within a row; in each aligned block of 128 rows (0 to 127, 128 to 255, ...) at most 10 rows name the same one
- gate_probs: float32 [16384, 8], P(('dp', 'tensor')), may hold values from 0.25 to 1
- expert_gate: bfloat16 [128, 4096, 768], P(('dp', 'tensor')), may hold values from -0.09375 to 0.09375
- expert_up: bfloat16 [128, 4096, 768], P(('dp', 'tensor')), may hold values from -0.09375 to 0.09375
- expert_down: bfloat16 [128, 768, 4096], P(('dp', 'tensor')), may hold values from -0.21875 to 0.21875
Outputs:
- layer_out: bfloat16 [16384, 4096], P(('dp', 'tensor'))
Inputs may be any that keep to these rules, and one draw needn't show every extreme that they name: `expert_ids`: each row names 8 different experts. Among the rows of one device (aligned blocks of 128 rows), no expert is named by more than 10 rows, a bound that some block reaches.
All inputs are finite; a program needn't handle non-finite values.
Results may differ from a plain program's by a relative error of at most 0.02.
Values may be sent and summed in bfloat16 or wider, within the bound.
No kernel may reach another device: no remote copies, remote signals or barrier semaphores. Data moves between devices by JAX's collectives and lax.ppermute only.
A program may use at most 128 MiB of HBM per device.

v0:
```python
import jax
import jax.numpy as jnp
from jax import lax
from jax.sharding import PartitionSpec as P

F32, BF16 = jnp.float32, jnp.bfloat16
MAIN = 8
QUARTERS = 4


def route(expert_ids, gate_probs, experts):
    toks = expert_ids.shape[0]
    names = jnp.arange(experts, dtype=jnp.int32)
    chosen = expert_ids.T[:, None, :] == names[None, :, None]
    taken = jnp.any(chosen, axis=0)
    prob = jnp.sum(jnp.where(chosen, gate_probs.T[:, None, :], 0.0), axis=0)
    order = jnp.arange(toks)
    earlier = (order[:, None] < order[None, :]).astype(BF16)
    before = jnp.dot(taken.astype(BF16), earlier, preferred_element_type=F32)
    return jnp.where(taken, before.astype(jnp.int32), -1), prob


def expert_apply(rows, w_gate, w_up, w_down):
    gate_act = jnp.dot(rows, w_gate, preferred_element_type=F32)
    up_act = jnp.dot(rows, w_up, preferred_element_type=F32)
    active = (jax.nn.silu(gate_act) * up_act).astype(BF16)
    return jnp.dot(active, w_down, preferred_element_type=F32).astype(BF16)


def shards(attn_heads, out_weight, residual, norm_gain, expert_ids, gate_probs, expert_gate, expert_up, expert_down):
    toks, width = residual.shape
    axes = ("dp", "tensor")
    experts = lax.axis_size("dp") * lax.axis_size("tensor")
    quarter = width // QUARTERS
    slot, prob = route(expert_ids, gate_probs, experts)
    row = jnp.arange(MAIN, dtype=jnp.int32)
    main_hot = slot[:, None, :] == row[None, :, None]
    spill_hot = slot[:, None, :] == (MAIN + row // QUARTERS)[None, :, None]
    piece = (row % QUARTERS)[None, :, None]
    spill_parts = [spill_hot & (piece == c) for c in range(QUARTERS)]

    attn_out = lax.psum_scatter(
        jnp.dot(attn_heads, out_weight, preferred_element_type=F32).astype(BF16),
        "tensor",
        scatter_dimension=0,
        tiled=True,
    ).astype(F32)
    hidden_state = residual.astype(F32) + attn_out
    inv_rms = lax.rsqrt(jnp.mean(hidden_state * hidden_state, axis=1, keepdims=True) + 1e-06)
    normed = (hidden_state * inv_rms * norm_gain).astype(BF16)

    flat = experts * MAIN
    main_out = jnp.dot(main_hot.reshape(flat, toks).astype(BF16), normed, preferred_element_type=F32).astype(BF16)
    stacked = jnp.concatenate([normed[:, c * quarter : (c + 1) * quarter] for c in range(QUARTERS)], axis=0)
    spill_all = jnp.concatenate([s.reshape(flat, toks) for s in spill_parts], axis=1).astype(BF16)
    spill_out = jnp.dot(spill_all, stacked, preferred_element_type=F32).astype(BF16)

    def swap(x, cols):
        y = lax.all_to_all(x.reshape(experts, MAIN, cols), axes, split_axis=0, concat_axis=0, tiled=True)
        return y.reshape(flat, cols)

    main_in = swap(main_out, width)
    spill_in = swap(spill_out, quarter)
    w = (expert_gate[0], expert_up[0], expert_down[0])
    main_back = swap(expert_apply(main_in, *w), width)
    spill_back = swap(expert_apply(spill_in.reshape(-1, width), *w).reshape(flat, quarter), quarter)

    hi = prob.astype(BF16)
    lo = (prob - hi.astype(F32)).astype(BF16)
    both = jnp.concatenate([hi, lo], axis=1)

    def combine(hot, rows):
        hot2 = jnp.concatenate([hot, hot], axis=2)
        weight = jnp.where(hot2, both[:, None, :], jnp.zeros((), BF16)).reshape(flat, 2 * toks)
        out = lax.dot_general(weight, rows, (((0,), (0,)), ((), ())), preferred_element_type=F32)
        return out[:toks] + out[toks:]

    routed = combine(main_hot, main_back)
    routed = routed + jnp.concatenate([combine(s, spill_back) for s in spill_parts], axis=1)
    return (hidden_state + routed).astype(BF16)


def solution(mesh):
    both = ("dp", "tensor")
    in_specs = (
        P("dp", "tensor"),
        P("tensor", None),
        P(both, None),
        P(),
        P(both, None),
        P(both, None),
        P(both, None, None),
        P(both, None, None),
        P(both, None, None),
    )
    return jax.shard_map(shards, mesh=mesh, in_specs=in_specs, out_specs=P(both, None), check_vma=False)
```

profile of v0, /device:TPU:1, one launch (start us, length us, event | category | flops | bytes accessed | tf_op | source)
XLA Modules:
  0.0 451.6 jit_solution(10391966449178340772)
XLA Ops:
  6.5 1.2 copy-done
  7.8 8.9 %convolution_convert_fusion = bf16[1024,4096]{1,0:T(8,128)(2,1)} fusion(bf16[1024,512]{1,0:T(8,128)(2,1)S(1)} %copy-done, bf16[512,4096]{1,0:T(8,128)(2,1)} %param.10), kind=kOutput, calls=%fused_computation.6 | convolution fusion | flops 4299161600 | bytes 13631488 | tf_op jit(solution)/shard_map/dot_general | solution.py:43
  16.6 0.0 reduce-scatter.2.cloned.1.call-update
  16.7 0.0 copy-start.8
  16.7 0.1 eq.117
  16.8 0.1 and.129
  17.0 0.1 and.141
  17.1 0.1 and.137
  17.2 0.1 and.133
  17.3 0.0 copy-done.9
  17.3 0.1 fusion.53
  17.4 0.1 fusion.39
  17.5 1.2 fusion.50
  18.8 115.4 %reduce-scatter.2.cloned.1.call-done = bf16[128,4096]{1,0:T(8,128)(2,1)} async-done(((bf16[1024,4096]{1,0:T(8,128)(2,1)}), bf16[128,4096]{1,0:T(8,128)(2,1)}) %reduce-scatter.2.cloned.1.call-update) | async-done | bytes 1048592 | tf_op jit(solution)/shard_map/reduce_scatter | solution.py:42
  134.2 1.7 multiply_reduce_fusion
  136.0 0.4 multiply_convert_fusion.1
  136.4 0.1 fusion.82
  136.5 2.6 convert_bitcast_fusion.2
  139.1 7.0 %all-to-all-start.2 = ((bf16[128,8,1024]{2,1,0:T(8,128)(2,1)}), bf16[128,8,1024]{2,1,0:T(8,128)(2,1)}, u32[]{:S(2)}, u32[]{:S(2)}) async-start(bf16[128,8,1024]{2,1,0:T(8,128)(2,1)} %convert_bitcast_fusion.2), calls=%async_computation.3 | async-start | bytes 4194304 | tf_op jit(solution)/shard_map/all_to_all | solution.py:59
  146.1 0.1 eq.110
  146.2 5.6 %convert_bitcast_fusion.1 = bf16[128,8,4096]{2,1,0:T(8,128)(2,1)} fusion(bf16[128,4096]{1,0:T(8,128)(2,1)S(1)} %multiply_convert_fusion.1, s32[1024]{0:T(1024)S(1)} %eq.110, s32[128,128]{1,0:T(8,128)S(1)} %fusion.39), kind=kOutput, calls=%fused_computation.5 | convolution fusion | flops 1078067200 | bytes 9506816 | tf_op jit(solution)/shard_map/dot_general | solution.py:53
  151.8 22.6 %all-to-all-done.2 = bf16[128,8,1024]{2,1,0:T(8,128)(2,1)} async-done(((bf16[128,8,1024]{2,1,0:T(8,128)(2,1)}), bf16[128,8,1024]{2,1,0:T(8,128)(2,1)}, u32[]{:S(2)}, u32[]{:S(2)}) %all-to-all-start.2) | async-done | bytes 2097184 | tf_op jit(solution)/shard_map/all_to_all | solution.py:59
  174.4 6.3 %all-to-all-start = ((bf16[128,8,4096]{2,1,0:T(8,128)(2,1)}), bf16[128,8,4096]{2,1,0:T(8,128)(2,1)}, u32[]{:S(2)}, u32[]{:S(2)}) async-start(bf16[128,8,4096]{2,1,0:T(8,128)(2,1)} %convert_bitcast_fusion.1), calls=%async_computation.1 | async-start | bytes 16777216 | tf_op jit(solution)/shard_map/all_to_all | solution.py:59
  180.7 0.1 select_reduce_fusion
  180.8 3.1 reshape_reshape.6
  183.9 4.6 %fusion.10 = f32[256,768]{1,0:T(8,128)S(1)} fusion(bf16[256,4096]{1,0:T(8,128)(2,1)S(1)} %reshape_reshape.6, bf16[1,4096,768]{2,1,0:T(8,128)(2,1)} %param.15), kind=kOutput, calls=%fused_computation.13 | convolution fusion | flops 1610612736 | bytes 9175040 | tf_op jit(solution)/shard_map/dot_general | solution.py:24
  188.5 10.5 %fusion.13 = bf16[256,4096]{1,0:T(8,128)(2,1)} fusion(bf16[1,768,4096]{2,1,0:T(8,128)(2,1)} %param.17, bf16[256,4096]{1,0:T(8,128)(2,1)S(1)} %reshape_reshape.6, bf16[1,4096,768]{2,1,0:T(8,128)(2,1)} %param.16, f32[256,768]{1,0:T(8,128)S(1)} %fusion.10), kind=kOutput, calls=%fused_computation.17 | convolution fusion | flops 3223453696 | bytes 17563648 | tf_op jit(solution)/shard_map/dot_general | solution.py:27
  199.0 4.4 reshape_reshape.7
  203.3 79.5 %all-to-all-done = bf16[128,8,4096]{2,1,0:T(8,128)(2,1)} async-done(((bf16[128,8,4096]{2,1,0:T(8,128)(2,1)}), bf16[128,8,4096]{2,1,0:T(8,128)(2,1)}, u32[]{:S(2)}, u32[]{:S(2)}) %all-to-all-start) | async-done | bytes 8388640 | tf_op jit(solution)/shard_map/all_to_all | solution.py:59
  282.9 10.2 %all-to-all-start.3 = ((bf16[128,8,1024]{2,1,0:T(8,128)(2,1)}), bf16[128,8,1024]{2,1,0:T(8,128)(2,1)S(1)}, u32[]{:S(2)}, u32[]{:S(2)}) async-start(bf16[128,8,1024]{2,1,0:T(8,128)(2,1)} %reshape_reshape.7), calls=%async_computation.4 | async-start | bytes 4194304 | tf_op jit(solution)/shard_map/all_to_all | solution.py:59
  293.1 0.0 slice-start
  293.1 11.0 %fusion = f32[1024,768]{1,0:T(8,128)S(1)} fusion(bf16[128,8,4096]{2,1,0:T(8,128)(2,1)} %all-to-all-done, bf16[1,4096,768]{2,1,0:T(8,128)(2,1)} %param.16), kind=kOutput, calls=%fused_computation | convolution fusion | flops 6442450944 | bytes 17825792 | tf_op jit(solution)/shard_map/dot_general | solution.py:25
  304.1 0.0 slice-start.1
  304.2 11.4 %multiply_convert_fusion = bf16[1024,768]{1,0:T(8,128)(2,1)S(1)} fusion(f32[1024,768]{1,0:T(8,128)S(1)} %fusion, bf16[1,4096,768]{2,1,0:T(8,128)(2,1)} %param.15, bf16[128,8,4096]{2,1,0:T(8,128)(2,1)} %all-to-all-done), kind=kOutput, calls=%fused_computation.18 | convolution fusion | flops 6447169536 | bytes 19398656 | tf_op jit(solution)/shard_map/dot_general | solution.py:24
  315.6 9.0 %convert_bitcast_fusion = bf16[128,8,4096]{2,1,0:T(8,128)(2,1)} fusion(bf16[1024,768]{1,0:T(8,128)(2,1)S(1)} %multiply_convert_fusion, bf16[1,768,4096]{2,1,0:T(8,128)(2,1)S(1)} %bitcast.78), kind=kOutput, calls=%fused_computation.4 | convolution fusion | flops 6446645248 | bytes 16252928 | tf_op jit(solution)/shard_map/dot_general | solution.py:27
  324.5 10.2 %all-to-all-start.1 = ((bf16[128,8,4096]{2,1,0:T(8,128)(2,1)}), bf16[128,8,4096]{2,1,0:T(8,128)(2,1)}, u32[]{:S(2)}, u32[]{:S(2)}) async-start(bf16[128,8,4096]{2,1,0:T(8,128)(2,1)} %convert_bitcast_fusion), calls=%async_computation.2 | async-start | bytes 16777216 | tf_op jit(solution)/shard_map/all_to_all | solution.py:59
  334.8 0.4 compare_and_fusion.3
  335.2 0.8 convolution_bitcast_fusion.1
  336.0 0.1 slice_add_fusion.1
  336.0 2.5 convolution_bitcast_fusion.2
  338.6 0.1 slice_add_fusion.2
  338.7 0.8 convolution_bitcast_fusion.3
  339.5 0.1 slice_add_fusion.3
  339.6 0.8 convolution_bitcast_fusion.4
  340.4 0.1 slice_add_fusion.4
  340.4 96.3 %all-to-all-done.1 = bf16[128,8,4096]{2,1,0:T(8,128)(2,1)} async-done(((bf16[128,8,4096]{2,1,0:T(8,128)(2,1)}), bf16[128,8,4096]{2,1,0:T(8,128)(2,1)}, u32[]{:S(2)}, u32[]{:S(2)}) %all-to-all-start.1) | async-done | bytes 8388640 | tf_op jit(solution)/shard_map/all_to_all | solution.py:59
  436.7 6.2 %convolution_bitcast_fusion = f32[256,4096]{1,0:T(8,128)S(1)} fusion(bf16[128,8,4096]{2,1,0:T(8,128)(2,1)} %all-to-all-done.1, pred[128,8,128]{2,1,0:T(8,128)(4,1)S(1)} %get-tuple-element.19, bf16[128,256]{1,0:T(8,128)(2,1)S(1)} %pad_maximum_fusion), kind=kOutput, calls=%fused_computation.16 | convolution fusion | flops 2148007936 | bytes 12779520 | tf_op jit(solution)/shard_map/dot_general | solution.py:75
  443.0 1.7 fusion.22
  (36 shorter events, 0.1 us)
Async XLA Ops:
  6.5 1.2 copy-start
  6.5 127.7 %reduce-scatter.2.cloned.1.call-start = ((), (), s32[]{:S(2)}) async-start(), calls=%async_computation.5 | async-start | bytes 9437184 | tf_op jit(solution)/shard_map/reduce_scatter | solution.py:42
  16.6 0.7 copy-start.9
  16.6 117.5 %copy-start.2 = (bf16[128,4096]{1,0:T(8,128)(2,1)S(1)}, bf16[128,4096]{1,0:T(8,128)(2,1)}, u32[]{:S(2)}) copy-start(bf16[128,4096]{1,0:T(8,128)(2,1)} %param.11) | copy-start | bytes 3145732
  16.7 119.3 %copy-start.8 = (f32[4096]{0:T(1024)S(1)}, f32[4096]{0:T(1024)}, u32[]{:S(2)}) copy-start(f32[4096]{0:T(1024)} %param.12) | copy-start | bytes 49156
  134.2 1.8 copy-start.4
  139.1 35.3 %all-to-all-start.2 = ((bf16[128,8,1024]{2,1,0:T(8,128)(2,1)}), bf16[128,8,1024]{2,1,0:T(8,128)(2,1)}, u32[]{:S(2)}, u32[]{:S(2)}) async-start(bf16[128,8,1024]{2,1,0:T(8,128)(2,1)} %convert_bitcast_fusion.2), calls=%async_computation.3 | async-start | bytes 4194304 | tf_op jit(solution)/shard_map/all_to_all | solution.py:59
  151.8 28.9 %copy-start.10 = (f32[128,8]{0,1:T(8,128)S(1)}, f32[128,8]{0,1:T(8,128)}, u32[]{:S(2)}) copy-start(f32[128,8]{0,1:T(8,128)} %param.14) | copy-start | bytes 12292
  174.4 108.4 %all-to-all-start = ((bf16[128,8,4096]{2,1,0:T(8,128)(2,1)}), bf16[128,8,4096]{2,1,0:T(8,128)(2,1)}, u32[]{:S(2)}, u32[]{:S(2)}) async-start(bf16[128,8,4096]{2,1,0:T(8,128)(2,1)} %convert_bitcast_fusion.1), calls=%async_computation.1 | async-start | bytes 16777216 | tf_op jit(solution)/shard_map/all_to_all | solution.py:59
  282.9 41.7 %all-to-all-start.3 = ((bf16[128,8,1024]{2,1,0:T(8,128)(2,1)}), bf16[128,8,1024]{2,1,0:T(8,128)(2,1)S(1)}, u32[]{:S(2)}, u32[]{:S(2)}) async-start(bf16[128,8,1024]{2,1,0:T(8,128)(2,1)} %reshape_reshape.7), calls=%async_computation.4 | async-start | bytes 4194304 | tf_op jit(solution)/shard_map/all_to_all | solution.py:59
  293.1 22.5 %slice-start = ((s8[6291456]{0:T(1024)(128)(4,1)}), s8[4194304]{0:T(1024)(128)(4,1)S(1)}, s32[]{:S(2)}) async-start(s8[6291456]{0:T(1024)(128)(4,1)} %bitcast.77), calls=%async_computation.6 | async-start | bytes 8388608
  304.1 11.4 %slice-start.1 = ((s8[6291456]{0:T(1024)(128)(4,1)}), s8[2097152]{0:T(1024)(128)(4,1)S(1)}, s32[]{:S(2)}) async-start(s8[6291456]{0:T(1024)(128)(4,1)} %bitcast.77), calls=%async_computation.7 | async-start | bytes 4194304
  324.5 10.6 %copy-start.6 = (bf16[128,8,1024]{2,1,0:T(8,128)(2,1)}, bf16[128,8,1024]{2,1,0:T(8,128)(2,1)S(1)}, u32[]{:S(2)}) copy-start(bf16[128,8,1024]{2,1,0:T(8,128)(2,1)S(1)} %all-to-all-done.3) | copy-start | bytes 6291460
  324.5 112.2 %all-to-all-start.1 = ((bf16[128,8,4096]{2,1,0:T(8,128)(2,1)}), bf16[128,8,4096]{2,1,0:T(8,128)(2,1)}, u32[]{:S(2)}, u32[]{:S(2)}) async-start(bf16[128,8,4096]{2,1,0:T(8,128)(2,1)} %convert_bitcast_fusion), calls=%async_computation.2 | async-start | bytes 16777216 | tf_op jit(solution)/shard_map/all_to_all | solution.py:59
  336.0 2.6 copy-start.7
  436.7 6.2 %copy-start.3 = (bf16[128,4096]{1,0:T(8,128)(2,1)S(1)}, bf16[128,4096]{1,0:T(8,128)(2,1)}, u32[]{:S(2)}) copy-start(bf16[128,4096]{1,0:T(8,128)(2,1)} %param.11) | copy-start | bytes 3145732
  436.7 6.2 %copy-start.5 = (bf16[128,4096]{1,0:T(8,128)(2,1)S(1)}, bf16[128,4096]{1,0:T(8,128)(2,1)}, u32[]{:S(2)}) copy-start(bf16[128,4096]{1,0:T(8,128)(2,1)} %reduce-scatter.2.cloned.1.call-done) | copy-start | bytes 3145732
  443.0 1.7 copy-start.1
Sparse Core Ops, SparseCore 0:
  16.8 117.3 reduce-scatter.1
where the time goes:
time: 455 us; the launch traced here: 452 us
  waiting for transfers between devices  314 us (69%)
  matrix products  74.9 us (16%)
  starting transfers between devices  33.7 us (7%)
  between operations  13.8 us (3%)
  local copies, waits for them, and re-layouts  9.51 us (2%)
  other arithmetic  5.85 us (1%)
    all_to_all x4, waiting for transfers between devices, swap(): lax.all_to_all(x.reshape(experts, MAIN, cols), axes, split_axis=0, concat...  198 us
    reduce_scatter x1, waiting for transfers between devices, shards(): lax.psum_scatter(jnp.dot(attn_heads, out_weight, preferred_element_type=F...  115 us
    all_to_all x4, starting transfers between devices, swap(): lax.all_to_all(x.reshape(experts, MAIN, cols), axes, split_axis=0, concat...  33.7 us
    dot_general x2, matrix products, expert_apply(): return jnp.dot(active, w_down, preferred_element_type=F32).astype(BF16)  19.4 us
    dot_general x2, matrix products, expert_apply(): gate_act = jnp.dot(rows, w_gate, preferred_element_type=F32)  15.9 us
    dot_general x5, matrix products, combine(): lax.dot_general(weight, rows, (((0,), (0,)), ((), ())), preferred_element...  11.2 us
    dot_general x1, matrix products, expert_apply(): up_act = jnp.dot(rows, w_up, preferred_element_type=F32)  11 us
  transfers between devices with their start and end apart: 5, of which 4 were waited for; matrix products, arithmetic and copies ran while one was open for 15% of the time, Pallas kernels for 0%

commit v1 on v0

v1 whole, which is shorter than its diff:
```python
import jax
import jax.numpy as jnp
from jax import lax
from jax.experimental import pallas as pl
from jax.experimental.pallas import tpu as pltpu
from jax.sharding import PartitionSpec as P

F32, BF16 = jnp.float32, jnp.bfloat16
MAIN = 8
PIECES = 4
VMEM = 40 * 2**20


def dot(a, b):
    return jnp.dot(a, b, preferred_element_type=F32)


def route(expert_ids, gate_probs, experts):
    toks = expert_ids.shape[0]
    names = jnp.arange(experts, dtype=jnp.int32)
    chosen = expert_ids.T[:, None, :] == names[None, :, None]
    taken = jnp.any(chosen, axis=0)
    prob = jnp.sum(jnp.where(chosen, gate_probs.T[:, None, :], 0.0), axis=0)
    order = jnp.arange(toks)
    earlier = (order[:, None] < order[None, :]).astype(BF16)
    before = dot(taken.astype(BF16), earlier)
    return jnp.where(taken, before.astype(jnp.int32), -1), prob


def combine_weights(slot, prob):
    experts, toks = slot.shape
    hi = prob.astype(BF16)
    lo = (prob - hi.astype(F32)).astype(BF16)
    both = jnp.concatenate([hi, lo], axis=1)
    row = jnp.arange(MAIN, dtype=jnp.int32)

    def spread(names):
        hot = slot[:, None, :] == names[None, :, None]
        hot = jnp.concatenate([hot, hot], axis=2)
        return jnp.where(hot, both[:, None, :], jnp.zeros((), BF16)).reshape(experts * MAIN, 2 * toks).T

    return spread(row), spread(MAIN + row // PIECES)


def build(slot, near, far, residual, gain):
    experts, toks = slot.shape
    width = residual.shape[1]
    tile = width // PIECES
    flat = experts * MAIN
    first = near.shape[1]

    def kernel(slot_ref, near_ref, far_ref, residual_ref, gain_ref, out_ref, hidden_ref, normed):
        step = pl.program_id(0)

        @pl.when(step == 0)
        def _():
            hidden_ref[:, :first] = residual_ref[:, :first].astype(F32) + near_ref[...]
            hidden_ref[:, first:] = residual_ref[:, first:].astype(F32) + far_ref[...]
            hidden = hidden_ref[...]
            inv_rms = lax.rsqrt(jnp.mean(hidden * hidden, axis=1, keepdims=True) + 1e-06)
            value = (hidden * inv_rms * gain_ref[...]).astype(BF16)
            for c in range(PIECES):
                normed[c] = value[:, c * tile : (c + 1) * tile]

        slots = jnp.broadcast_to(slot_ref[...][:, None, :], (experts, MAIN, toks))
        row = lax.broadcasted_iota(jnp.int32, (experts, MAIN, toks), 1)

        def hot(mask):
            return jnp.where(mask, 1.0, 0.0).reshape(flat, toks).astype(BF16)

        @pl.when(step < PIECES)
        def _():
            out_ref[...] = dot(hot(slots == row), normed[step]).astype(BF16)

        @pl.when(step == PIECES)
        def _():
            spill = slots == MAIN + row // PIECES
            total = jnp.zeros((flat, tile), F32)
            for c in range(PIECES):
                total = total + dot(hot(spill & (row % PIECES == c)), normed[c])
            out_ref[...] = total.astype(BF16)

    whole = lambda i: (0, 0)
    return pl.pallas_call(
        kernel,
        grid=(PIECES + 1,),
        in_specs=[
            pl.BlockSpec(slot.shape, whole),
            pl.BlockSpec(near.shape, whole),
            pl.BlockSpec(far.shape, whole),
            pl.BlockSpec(residual.shape, whole),
            pl.BlockSpec(gain.shape, whole),
        ],
        out_specs=[pl.BlockSpec((flat, tile), lambda i: (0, i)), pl.BlockSpec((toks, width), whole)],
        out_shape=[
            jax.ShapeDtypeStruct((flat, tile * (PIECES + 1)), BF16),
            jax.ShapeDtypeStruct((toks, width), F32),
        ],
        scratch_shapes=[pltpu.VMEM((PIECES, toks, tile), BF16)],
        compiler_params=pltpu.CompilerParams(vmem_limit_bytes=VMEM),
        cost_estimate=pl.CostEstimate(flops=3 * 10**9, bytes_accessed=15 * 10**6, transcendentals=0),
        name="build_rows",
    )(slot, near, far, residual, gain)


def silu_times(gate, up):
    return (gate * jax.nn.sigmoid(gate) * up).astype(BF16)


def spill_expert(got, w_gate, w_up, w_down):
    flat, columns = got.shape
    hid = w_gate.shape[1]
    tile = columns // (PIECES + 1)
    rows = flat // PIECES

    def picks(c, shape, out_dim):
        out = lax.broadcasted_iota(jnp.int32, shape, out_dim)
        source = lax.broadcasted_iota(jnp.int32, shape, 1 - out_dim)
        return jnp.where(source == out * PIECES + c, 1.0, 0.0).astype(BF16)

    def kernel(got_ref, gate_ref, up_ref, down_ref, out_ref, gate_sum, up_sum, active, total):
        step = pl.program_id(0)

        @pl.when(step == 0)
        def _():
            gate_sum[...] = jnp.zeros_like(gate_sum)
            up_sum[...] = jnp.zeros_like(up_sum)
            total[...] = jnp.zeros_like(total)

        @pl.when(step < PIECES)
        def _():
            value = dot(picks(step, (rows, flat), 0), got_ref[...]).astype(BF16)
            gate_sum[...] += dot(value, gate_ref[...])
            up_sum[...] += dot(value, up_ref[...])

        @pl.when(step == PIECES)
        def _():
            active[...] = silu_times(gate_sum[...], up_sum[...])

        @pl.when(step >= PIECES)
        def _():
            value = dot(active[...], down_ref[...]).astype(BF16)
            total[...] += dot(picks(step - PIECES, (flat, rows), 1), value)

        @pl.when(step == 2 * PIECES - 1)
        def _():
            out_ref[...] = total[...].astype(BF16)

    early = lambda i: (jnp.minimum(i, PIECES - 1), 0)
    return pl.pallas_call(
        kernel,
        grid=(2 * PIECES,),
        in_specs=[
            pl.BlockSpec((flat, tile), lambda i: (0, PIECES)),
            pl.BlockSpec((tile, hid), early),
            pl.BlockSpec((tile, hid), early),
            pl.BlockSpec((hid, tile), lambda i: (0, jnp.maximum(i - PIECES, 0))),
        ],
        out_specs=pl.BlockSpec((flat, tile), lambda i: (0, 0)),
        out_shape=jax.ShapeDtypeStruct((flat, tile), BF16),
        scratch_shapes=[
            pltpu.VMEM((rows, hid), F32),
            pltpu.VMEM((rows, hid), F32),
            pltpu.VMEM((rows, hid), BF16),
            pltpu.VMEM((flat, tile), F32),
        ],
        compiler_params=pltpu.CompilerParams(vmem_limit_bytes=63 * 2**20),
        cost_estimate=pl.CostEstimate(flops=9 * 10**9, bytes_accessed=23 * 10**6, transcendentals=0),
        name="spill_expert",
    )(got, w_gate, w_up, w_down)


def main_expert(got, w_gate, w_up, w_down):
    width, hid = w_gate.shape
    flat = got.shape[0]
    block = 256

    def kernel(rows_ref, gate_ref, up_ref, down_ref, out_ref):
        rows = rows_ref[...]
        active = silu_times(dot(rows, gate_ref[...]), dot(rows, up_ref[...]))
        out_ref[...] = dot(active, down_ref[...]).astype(BF16)

    whole = lambda i: (0, 0)
    once = pl.Buffered(1)
    return pl.pallas_call(
        kernel,
        grid=(flat // block,),
        in_specs=[
            pl.BlockSpec((block, width), lambda i: (i, 0)),
            pl.BlockSpec((width, hid), whole, pipeline_mode=once),
            pl.BlockSpec((width, hid), whole, pipeline_mode=once),
            pl.BlockSpec((hid, width), whole, pipeline_mode=once),
        ],
        out_specs=pl.BlockSpec((block, width), lambda i: (i, 0)),
        out_shape=jax.ShapeDtypeStruct((flat, width), BF16),
        compiler_params=pltpu.CompilerParams(vmem_limit_bytes=VMEM),
        cost_estimate=pl.CostEstimate(flops=20 * 10**9, bytes_accessed=36 * 10**6, transcendentals=10**6),
        name="main_expert",
    )(got, w_gate, w_up, w_down)


def combine(main_w, spill_w, main_rows, spill_rows, hidden):
    toks, width = hidden.shape
    flat = main_rows.shape[0]
    quarter = spill_rows.shape[1]
    halves = 2
    tile = quarter // halves

    def kernel(main_w_ref, spill_w_ref, main_ref, spill_ref, hidden_ref, out_ref):
        piece = pl.program_id(0) // halves
        column = lax.broadcasted_iota(jnp.int32, (2 * toks, flat), 1)
        spill = jnp.where(column % PIECES == piece, spill_w_ref[...].astype(F32), 0.0).astype(BF16)
        both = dot(main_w_ref[...], main_ref[...]) + dot(spill, spill_ref[...])
        out_ref[...] = (hidden_ref[...] + (both[:toks] + both[toks:])).astype(BF16)

    whole = lambda i: (0, 0)
    along = lambda i: (0, i)
    return pl.pallas_call(
        kernel,
        grid=(PIECES * halves,),
        in_specs=[
            pl.BlockSpec((2 * toks, flat), whole),
            pl.BlockSpec((2 * toks, flat), whole),
            pl.BlockSpec((flat, tile), along),
            pl.BlockSpec((flat, tile), lambda i: (0, i % halves)),
            pl.BlockSpec((toks, tile), along),
        ],
        out_specs=pl.BlockSpec((toks, tile), along),
        out_shape=jax.ShapeDtypeStruct((toks, width), BF16),
        compiler_params=pltpu.CompilerParams(vmem_limit_bytes=VMEM),
        cost_estimate=pl.CostEstimate(flops=4 * 10**9, bytes_accessed=15 * 10**6, transcendentals=0),
        name="combine_rows",
    )(main_w, spill_w, main_rows, spill_rows, hidden)


def project_scatter(attn_heads, out_weight, toks):
    width = out_weight.shape[1]
    first = width * 5 // 8
    at = lax.axis_index("tensor")
    x, z = at // 2, at % 2
    heads = attn_heads.reshape(4, 2, toks, attn_heads.shape[1])

    def along_x(v, by):
        return lax.ppermute(v, "tensor", [(i * 2 + j, (i + by) % 4 * 2 + j) for i in range(4) for j in range(2)])

    def along_z(v):
        return lax.ppermute(v, "tensor", [(i, i ^ 1) for i in range(8)])

    def times(rows, lo, hi):
        return dot(rows, out_weight[:, lo:hi]).astype(BF16)

    def pick(v, i):
        return lax.dynamic_index_in_dim(v, i, 0, keepdims=False)

    def add(a, b):
        return (a.astype(F32) + b.astype(F32)).astype(BF16)

    by_z = heads.swapaxes(0, 1)
    far_rows = [pick(heads, (x + d) % 4).reshape(2 * toks, -1) for d in range(4)]
    mid = first // 2

    up_two, down_two = times(far_rows[2], mid, first), times(far_rows[2], 0, mid)
    z_rows = pick(by_z, 1 - z).reshape(4 * toks, -1)
    up_two, down_two, z_rows = lax.optimization_barrier((up_two, down_two, z_rows))
    up_far, down_far = along_x(up_two, 1), along_x(down_two, -1)
    away = along_z(times(z_rows, first, width))
    up_near = along_x(times(far_rows[1], 0, mid), 1)
    down_near = along_x(times(far_rows[3], mid, first), -1)
    up_sum = along_x(add(dot(far_rows[1], out_weight[:, mid:first]).astype(BF16), up_far), 1)
    down_sum = along_x(add(dot(far_rows[3], out_weight[:, :mid]).astype(BF16), down_far), -1)

    own = times(pick(by_z, z).reshape(4 * toks, -1), first, width)
    both = add(own, away)
    both, own_rows = lax.optimization_barrier((both, far_rows[0]))
    both = both.reshape(4, toks, width - first)
    chunk = [pick(both, (x + d) % 4) for d in range(4)]
    half = (width - first) // 2
    b_up_far, b_down_far = along_x(chunk[2][:, half:], 1), along_x(chunk[2][:, :half], -1)
    b_up_near, b_down_near = along_x(chunk[1][:, :half], 1), along_x(chunk[3][:, half:], -1)
    b_up_sum = along_x(add(chunk[1][:, half:], b_up_far), 1)
    b_down_sum = along_x(add(chunk[3][:, :half], b_down_far), -1)

    left = times(own_rows, 0, mid).astype(F32) + up_near.astype(F32) + down_sum.astype(F32)
    right = times(own_rows, mid, first).astype(F32) + up_sum.astype(F32) + down_near.astype(F32)
    near = jnp.concatenate([left, right], axis=1).reshape(2, toks, first)
    near = pick(near, z) + along_z(pick(near, 1 - z).astype(BF16)).astype(F32)
    b_left = chunk[0][:, :half].astype(F32) + b_up_near.astype(F32) + b_down_sum.astype(F32)
    b_right = chunk[0][:, half:].astype(F32) + b_up_sum.astype(F32) + b_down_near.astype(F32)
    return near, jnp.concatenate([b_left, b_right], axis=1)


def shards(attn_heads, out_weight, residual, norm_gain, expert_ids, gate_probs, expert_gate, expert_up, expert_down):
    toks, width = residual.shape
    experts = lax.axis_size("dp") * lax.axis_size("tensor")
    flat = experts * MAIN
    slot, prob = route(expert_ids, gate_probs, experts)
    main_w, spill_w = combine_weights(slot, prob)
    near, far = project_scatter(attn_heads, out_weight, toks)
    sent, hidden = build(slot, near, far, residual, norm_gain[None, :])

    def swap(v):
        cols = v.shape[1]
        v = lax.all_to_all(v.reshape(experts, MAIN, cols), ("dp", "tensor"), split_axis=0, concat_axis=0, tiled=True)
        return v.reshape(flat, cols)

    got = swap(sent)
    w = (expert_gate[0], expert_up[0], expert_down[0])
    spill_out = spill_expert(got, *w)
    spill_out, got = lax.optimization_barrier((spill_out, got))
    spill_back = swap(spill_out)
    main_back = swap(main_expert(got, *w))
    return combine(main_w, spill_w, main_back, spill_back, hidden)


def solution(mesh):
    both = ("dp", "tensor")
    in_specs = (
        P("dp", "tensor"),
        P("tensor", None),
        P(both, None),
        P(),
        P(both, None),
        P(both, None),
        P(both, None, None),
        P(both, None, None),
        P(both, None, None),
    )
    return jax.shard_map(shards, mesh=mesh, in_specs=in_specs, out_specs=P(both, None), check_vma=False)
```

time: 455 us -> 398 us (0.87)
  waiting for transfers between devices: 314 us -> 137 us
  blocking collectives: 0 us -> 131 us
  matrix products: 74.9 us -> 10.5 us
  Pallas kernels: 0 us -> 60.6 us
  between operations: 13.8 us -> 0.44 us
  starting transfers between devices: 33.7 us -> 41 us
    all_to_all x0 -> x1, blocking collectives: none -> 131 us  [swap(): lax.all_to_all(v.reshape(experts, MAIN, cols), ('dp', 'tensor'), split_ax...]
    reduce_scatter x1 -> x0, waiting for transfers between devices: 115 us -> none  [shards(): lax.psum_scatter(jnp.dot(attn_heads, out_weight, preferred_element_type=F...]
    all_to_all x4 -> x2, waiting for transfers between devices: 198 us -> 99.8 us  [swap(): lax.all_to_all(v.reshape(experts, MAIN, cols), ('dp', 'tensor'), split_ax...]
    dot_general x14 -> x11, matrix products: 74.9 us -> 10.5 us  [dot(): return jnp.dot(a, b, preferred_element_type=F32)]
    pallas_call x0 -> x4, Pallas kernels: none -> 60.6 us  [the longest x1 25 us: main_expert(): pl.pallas_call(kernel, grid=(flat // block,), in_specs=[pl.BlockSpec((blo...]
    ppermute x0 -> x14, waiting for transfers between devices: none -> 37.3 us  [the longest x12 37.1 us: along_x(): lax.ppermute(v, 'tensor', [(i * 2 + j, (i + by) % 4 * 2 + j) for i in ran...]
    ppermute x0 -> x14, starting transfers between devices: none -> 23.4 us  [the longest x12 18.2 us: along_x(): lax.ppermute(v, 'tensor', [(i * 2 + j, (i + by) % 4 * 2 + j) for i in ran...]
    all_to_all x4 -> x2, starting transfers between devices: 33.7 us -> 17.6 us  [swap(): lax.all_to_all(v.reshape(experts, MAIN, cols), ('dp', 'tensor'), split_ax...]
  transfers between devices with their start and end apart: 5 -> 16, of which waited for: 4 -> 9; matrix products, arithmetic and copies ran while one was open for 15% -> 2% of each run, Pallas kernels for 0% -> 6%
where the time goes in v1:
time: 398 us; the launch traced here: 395 us
  waiting for transfers between devices  137 us (34%)
  blocking collectives  131 us (33%)
  Pallas kernels  60.6 us (15%)
  starting transfers between devices  41 us (10%)
  local copies, waits for them, and re-layouts  11.3 us (3%)
  matrix products  10.5 us (3%)
    all_to_all x1, blocking collectives, swap(): lax.all_to_all(v.reshape(experts, MAIN, cols), ('dp', 'tensor'), split_ax...  131 us
    all_to_all x2, waiting for transfers between devices, swap(): lax.all_to_all(v.reshape(experts, MAIN, cols), ('dp', 'tensor'), split_ax...  99.8 us
    ppermute x12, waiting for transfers between devices, along_x(): lax.ppermute(v, 'tensor', [(i * 2 + j, (i + by) % 4 * 2 + j) for i in ran...  37.1 us
    pallas_call x1, Pallas kernels, main_expert(): pl.pallas_call(kernel, grid=(flat // block,), in_specs=[pl.BlockSpec((blo...  25 us
    ppermute x12, starting transfers between devices, along_x(): lax.ppermute(v, 'tensor', [(i * 2 + j, (i + by) % 4 * 2 + j) for i in ran...  18.2 us
    all_to_all x2, starting transfers between devices, swap(): lax.all_to_all(v.reshape(experts, MAIN, cols), ('dp', 'tensor'), split_ax...  17.6 us
    pallas_call x1, Pallas kernels, spill_expert(): pl.pallas_call(kernel, grid=(2 * PIECES,), in_specs=[pl.BlockSpec((flat,...  17.2 us
    dot_general x11, matrix products, dot(): return jnp.dot(a, b, preferred_element_type=F32)  10.5 us
  transfers between devices with their start and end apart: 16, of which 9 were waited for; matrix products, arithmetic and copies ran while one was open for 2% of the time, Pallas kernels for 6%

profile of v1, /device:TPU:1, one launch (start us, length us, event | category | flops | bytes accessed | tf_op | source)
XLA Modules:
  0.0 394.5 jit_solution(9917804577058518395)
XLA Ops:
  0.0 1.3 constant_dynamic-slice_fusion.1
  1.3 1.8 convolution_convert_fusion.8
  3.1 1.9 convolution_convert_fusion.9
  5.2 2.5 convolution_convert_fusion
  7.7 4.5 %collective-permute-start = (bf16[512,1536]{1,0:T(8,128)(2,1)S(1)}, bf16[512,1536]{1,0:T(8,128)(2,1)S(1)}, u32[]{:S(2)}, u32[]{:S(2)}) collective-permute-start(bf16[512,1536]{1,0:T(8,128)(2,1)S(1)} %convolution_convert_fusion), channel_id=1, source_target_pairs={{0,1},{1,0},{2,3},{3,2},{4,5},{5,4},{6,7},{7,6},{8,9},{9,8},{10,11... | collective-permute-start | bytes 4718600 | tf_op jit(solution)/shard_map/ppermute | solution.py:247
  12.2 2.5 collective-permute-start.2
  14.7 0.5 convolution_convert_fusion.6
  15.3 0.2 collective-permute-start.4
  15.5 0.5 convolution_convert_fusion.2
  16.0 2.6 collective-permute-start.6
  18.7 9.1 %collective-permute-done.2 = bf16[256,1280]{1,0:T(8,128)(2,1)S(1)} collective-permute-done((bf16[256,1280]{1,0:T(8,128)(2,1)S(1)}, bf16[256,1280]{1,0:T(8,128)(2,1)S(1)}, u32[]{:S(2)}, u32[]{:S(2)}) %collective-permute-start.2) | collective-permute-done | bytes 655392 | tf_op jit(solution)/shard_map/ppermute | solution.py:244
  27.8 0.5 add_convert_fusion.2
  28.3 3.5 collective-permute-start.3
  31.8 13.8 %collective-permute-done.4 = bf16[256,1280]{1,0:T(8,128)(2,1)S(1)} collective-permute-done((bf16[256,1280]{1,0:T(8,128)(2,1)S(1)}, bf16[256,1280]{1,0:T(8,128)(2,1)S(1)}, u32[]{:S(2)}, u32[]{:S(2)}) %collective-permute-start.4) | collective-permute-done | bytes 655392 | tf_op jit(solution)/shard_map/ppermute | solution.py:244
  45.6 0.5 add_convert_fusion.1
  46.2 0.2 collective-permute-done
  46.4 1.0 add_convert_fusion
  47.4 0.5 fusion
  48.0 0.5 fusion.2
  48.6 1.3 collective-permute-start.11
  49.9 1.5 collective-permute-start.9
  51.5 4.4 %collective-permute-done.3 = bf16[256,1280]{1,0:T(8,128)(2,1)S(1)} collective-permute-done((bf16[256,1280]{1,0:T(8,128)(2,1)S(1)}, bf16[256,1280]{1,0:T(8,128)(2,1)S(1)}, u32[]{:S(2)}, u32[]{:S(2)}) %collective-permute-start.3) | collective-permute-done | bytes 655392 | tf_op jit(solution)/shard_map/ppermute | solution.py:244
  55.9 3.4 collective-permute-start.13
  59.3 0.2 convert_add_fusion.1
  59.6 1.8 collective-permute-done.5
  61.4 0.2 convert_add_fusion
  61.7 0.3 pad_maximum_fusion
  62.1 0.7 collective-permute-start.7
  62.8 2.8 collective-permute-done.11
  65.9 2.9 collective-permute-start.10
  68.9 0.9 collective-permute-done.8
  69.9 4.2 %collective-permute-done.12 = bf16[128,768]{1,0:T(8,128)(2,1)S(1)} collective-permute-done((bf16[128,768]{1,0:T(8,128)(2,1)S(1)}, bf16[128,768]{1,0:T(8,128)(2,1)S(1)}, u32[]{:S(2)}, u32[]{:S(2)}) %collective-permute-start.12) | collective-permute-done | bytes 196640 | tf_op jit(solution)/shard_map/ppermute | solution.py:244
  74.3 0.1 bitcast_add_fusion.near_ref
  74.5 1.0 copy-done.2
  75.5 8.8 %build_rows.1 = (bf16[1024,5120]{1,0:T(8,128)(2,1)}, f32[128,4096]{1,0:T(8,128)S(1)}) custom-call(s32[128,128]{1,0:T(8,128)S(1)} %fusion.6.slot_ref, f32[128,2560]{1,0:T(8,128)S(1)} %bitcast_add_fusion.near_ref, f32[128,1536]{1,0:T(8,128)S(1)} %pad_maximum_fusion.1.far_ref, bf16[128,4096]{1,0:T(8,128)(2,1)S(1)} %copy-done.2, f32[1,4096]{1,0:T(1,128)S(1)} %bitcast.57), custom_call_target="tpu_custom_call" | custom-call | flops 3000000000 | bytes 15000000 | tf_op jit(solution)/shard_map/build_rows/pallas_call | solution.py:84
  84.3 130.8 %all_to_all.15 = bf16[128,8,5120]{2,1,0:T(8,128)(2,1)} all-to-all(bf16[128,8,5120]{2,1,0:T(8,128)(2,1)} %bitcast.60), channel_id=1, replica_groups=mesh['dp'=16,'tensor'=8] {'dp','tensor'}, dimensions={0} | all-to-all | bytes 20971520 | tf_op jit(solution)/shard_map/all_to_all | solution.py:303
  215.1 17.2 %spill_expert.1 = bf16[1024,1024]{1,0:T(8,128)(2,1)} custom-call(bf16[1024,5120]{1,0:T(8,128)(2,1)} %bitcast.58, bf16[4096,768]{1,0:T(8,128)(2,1)} %bitcast.53, bf16[4096,768]{1,0:T(8,128)(2,1)} %bitcast.55, bf16[768,4096]{1,0:T(8,128)(2,1)} %bitcast.81), custom_call_target="tpu_custom_call" | custom-call | flops 8999999488 | bytes 23000000 | tf_op jit(solution)/shard_map/spill_expert/pallas_call | solution.py:150
  232.3 7.4 %all-to-all-start.2 = ((bf16[128,8,1024]{2,1,0:T(8,128)(2,1)}), bf16[128,8,1024]{2,1,0:T(8,128)(2,1)S(1)}, u32[]{:S(2)}, u32[]{:S(2)}) async-start(bf16[128,8,1024]{2,1,0:T(8,128)(2,1)} %bitcast.68), calls=%async_computation.2 | async-start | bytes 4194304 | tf_op jit(solution)/shard_map/all_to_all | solution.py:303
  239.7 2.8 copy-done
  242.5 2.8 copy-done.1
  245.3 25.0 %main_expert.1 = bf16[1024,4096]{1,0:T(8,128)(2,1)} custom-call(bf16[1024,5120]{1,0:T(8,128)(2,1)} %bitcast.59, bf16[4096,768]{1,0:T(8,128)(2,1)S(1)} %bitcast.54, bf16[4096,768]{1,0:T(8,128)(2,1)S(1)} %bitcast.56, bf16[768,4096]{1,0:T(8,128)(2,1)} %bitcast.82), custom_call_target="tpu_custom_call" | custom-call | flops 20000000000 | bytes 36000000 | tf_op jit(solution)/shard_map/main_expert/pallas_call | solution.py:185
  270.2 10.2 %all-to-all-start.1 = ((bf16[128,8,4096]{2,1,0:T(8,128)(2,1)}), bf16[128,8,4096]{2,1,0:T(8,128)(2,1)}, u32[]{:S(2)}, u32[]{:S(2)}) async-start(bf16[128,8,4096]{2,1,0:T(8,128)(2,1)} %bitcast.61), calls=%async_computation.1 | async-start | bytes 16777216 | tf_op jit(solution)/shard_map/all_to_all | solution.py:303
  280.7 1.0 copy.16
  281.7 0.2 copy.15
  282.3 1.1 fusion.20
  283.4 99.8 %all-to-all-done.1 = bf16[128,8,4096]{2,1,0:T(8,128)(2,1)} async-done(((bf16[128,8,4096]{2,1,0:T(8,128)(2,1)}), bf16[128,8,4096]{2,1,0:T(8,128)(2,1)}, u32[]{:S(2)}, u32[]{:S(2)}) %all-to-all-start.1) | async-done | bytes 8388640 | tf_op jit(solution)/shard_map/all_to_all | solution.py:303
  383.3 1.6 copy-done.5
  384.9 9.6 %combine_rows.1 = bf16[128,4096]{1,0:T(8,128)(2,1)} custom-call(bf16[256,1024]{1,0:T(8,128)(2,1)S(1)} %get-tuple-element.36.main_w_ref, bf16[256,1024]{1,0:T(8,128)(2,1)S(1)} %get-tuple-element.35.spill_w_ref, bf16[1024,4096]{1,0:T(8,128)(2,1)} %bitcast.28.main_ref, bf16[1024,1024]{1,0:T(8,128)(2,1)S(1)} %bitcast.52, f32[128,4096]{1,0:T(8,128)S(1)} %copy-done.5), custom_call_target="tpu_custom_call" | custom-call | flops 4000000000 | bytes 15000000 | tf_op jit(solution)/shard_map/combine_rows/pallas_call | solution.py:218
  (50 shorter events, 1.7 us)
Async XLA Ops:
  3.1 2.0 copy-start.6
  5.2 9.6 %copy-start.7 = (bf16[512,4096]{1,0:T(8,128)(2,1)S(1)}, bf16[512,4096]{1,0:T(8,128)(2,1)}, u32[]{:S(2)}) copy-start(bf16[512,4096]{1,0:T(8,128)(2,1)} %param.10) | copy-start | bytes 12582916
  7.7 38.6 %collective-permute-start = (bf16[512,1536]{1,0:T(8,128)(2,1)S(1)}, bf16[512,1536]{1,0:T(8,128)(2,1)S(1)}, u32[]{:S(2)}, u32[]{:S(2)}) collective-permute-start(bf16[512,1536]{1,0:T(8,128)(2,1)S(1)} %convolution_convert_fusion), channel_id=1, source_target_pairs={{0,1},{1,0},{2,3},{3,2},{4,5},{5,4},{6,7},{7,6},{8,9},{9,8},{10,11... | collective-permute-start | bytes 4718600 | tf_op jit(solution)/shard_map/ppermute | solution.py:247
  12.2 15.6 %collective-permute-start.2 = (bf16[256,1280]{1,0:T(8,128)(2,1)S(1)}, bf16[256,1280]{1,0:T(8,128)(2,1)S(1)}, u32[]{:S(2)}, u32[]{:S(2)}) collective-permute-start(bf16[256,1280]{1,0:T(8,128)(2,1)S(1)} %convolution_convert_fusion.8), channel_id=1, source_target_pairs={{0,6},{1,7},{2,0},{3,1},{4,2},{5,3},{6,4},{7,5},{8,14},{9,15},{10,... | collective-permute-start | bytes 1966088 | tf_op jit(solution)/shard_map/ppermute | solution.py:244
  15.2 3.4 copy-start.8
  15.3 34.7 %collective-permute-start.1 = (bf16[256,1280]{1,0:T(8,128)(2,1)S(1)}, bf16[256,1280]{1,0:T(8,128)(2,1)S(1)}, u32[]{:S(2)}, u32[]{:S(2)}) collective-permute-start(bf16[256,1280]{1,0:T(8,128)(2,1)S(1)} %convolution_convert_fusion.6), channel_id=1, source_target_pairs={{0,2},{1,3},{2,4},{3,5},{4,6},{5,7},{6,0},{7,1},{8,10},{9,11},{10,... | collective-permute-start | bytes 1966088 | tf_op jit(solution)/shard_map/ppermute | solution.py:244
  15.3 30.2 %collective-permute-start.4 = (bf16[256,1280]{1,0:T(8,128)(2,1)S(1)}, bf16[256,1280]{1,0:T(8,128)(2,1)S(1)}, u32[]{:S(2)}, u32[]{:S(2)}) collective-permute-start(bf16[256,1280]{1,0:T(8,128)(2,1)S(1)} %convolution_convert_fusion.9), channel_id=1, source_target_pairs={{0,2},{1,3},{2,4},{3,5},{4,6},{5,7},{6,0},{7,1},{8,10},{9,11},{10,... | collective-permute-start | bytes 1966088 | tf_op jit(solution)/shard_map/ppermute | solution.py:244
  16.0 43.5 %collective-permute-start.6 = (bf16[256,1280]{1,0:T(8,128)(2,1)S(1)}, bf16[256,1280]{1,0:T(8,128)(2,1)S(1)}, u32[]{:S(2)}, u32[]{:S(2)}) collective-permute-start(bf16[256,1280]{1,0:T(8,128)(2,1)S(1)} %convolution_convert_fusion.2), channel_id=1, source_target_pairs={{0,6},{1,7},{2,0},{3,1},{4,2},{5,3},{6,4},{7,5},{8,14},{9,15},{10,... | collective-permute-start | bytes 1966088 | tf_op jit(solution)/shard_map/ppermute | solution.py:244
  28.3 27.6 %collective-permute-start.3 = (bf16[256,1280]{1,0:T(8,128)(2,1)S(1)}, bf16[256,1280]{1,0:T(8,128)(2,1)S(1)}, u32[]{:S(2)}, u32[]{:S(2)}) collective-permute-start(bf16[256,1280]{1,0:T(8,128)(2,1)S(1)} %add_convert_fusion.2), channel_id=1, source_target_pairs={{0,6},{1,7},{2,0},{3,1},{4,2},{5,3},{6,4},{7,5},{8,14},{9,15},{10,... | collective-permute-start | bytes 1966088 | tf_op jit(solution)/shard_map/ppermute | solution.py:244
  46.1 15.3 %collective-permute-start.5 = (bf16[256,1280]{1,0:T(8,128)(2,1)S(1)}, bf16[256,1280]{1,0:T(8,128)(2,1)S(1)}, u32[]{:S(2)}, u32[]{:S(2)}) collective-permute-start(bf16[256,1280]{1,0:T(8,128)(2,1)S(1)} %add_convert_fusion.1), channel_id=1, source_target_pairs={{0,2},{1,3},{2,4},{3,5},{4,6},{5,7},{6,0},{7,1},{8,10},{9,11},{10,... | collective-permute-start | bytes 1966088 | tf_op jit(solution)/shard_map/ppermute | solution.py:244
  48.6 17.1 %collective-permute-start.11 = (bf16[128,768]{1,0:T(8,128)(2,1)S(1)}, bf16[128,768]{1,0:T(8,128)(2,1)S(1)}, u32[]{:S(2)}, u32[]{:S(2)}) collective-permute-start(bf16[128,768]{1,0:T(8,128)(2,1)S(1)} %get-tuple-element.42), channel_id=1, source_target_pairs={{0,2},{1,3},{2,4},{3,5},{4,6},{5,7},{6,0},{7,1},{8,10},{9,11},{10,... | collective-permute-start | bytes 589832 | tf_op jit(solution)/shard_map/ppermute | solution.py:244
  49.9 15.9 %collective-permute-start.9 = (bf16[128,768]{1,0:T(8,128)(2,1)S(1)}, bf16[128,768]{1,0:T(8,128)(2,1)S(1)}, u32[]{:S(2)}, u32[]{:S(2)}) collective-permute-start(bf16[128,768]{1,0:T(8,128)(2,1)S(1)} %get-tuple-element.41), channel_id=1, source_target_pairs={{0,6},{1,7},{2,0},{3,1},{4,2},{5,3},{6,4},{7,5},{8,14},{9,15},{10,... | collective-permute-start | bytes 589832 | tf_op jit(solution)/shard_map/ppermute | solution.py:244
  55.9 13.0 %collective-permute-start.13 = (bf16[128,768]{1,0:T(8,128)(2,1)S(1)}, bf16[128,768]{1,0:T(8,128)(2,1)S(1)}, u32[]{:S(2)}, u32[]{:S(2)}) collective-permute-start(bf16[128,768]{1,0:T(8,128)(2,1)S(1)} %slice.58), channel_id=1, source_target_pairs={{0,6},{1,7},{2,0},{3,1},{4,2},{5,3},{6,4},{7,5},{8,14},{9,15},{10,... | collective-permute-start | bytes 589832 | tf_op jit(solution)/shard_map/ppermute | solution.py:244
  59.5 10.3 %collective-permute-start.8 = (bf16[128,768]{1,0:T(8,128)(2,1)S(1)}, bf16[128,768]{1,0:T(8,128)(2,1)S(1)}, u32[]{:S(2)}, u32[]{:S(2)}) collective-permute-start(bf16[128,768]{1,0:T(8,128)(2,1)S(1)} %slice.52), channel_id=1, source_target_pairs={{0,2},{1,3},{2,4},{3,5},{4,6},{5,7},{6,0},{7,1},{8,10},{9,11},{10,... | collective-permute-start | bytes 589832 | tf_op jit(solution)/shard_map/ppermute | solution.py:244
  62.1 12.2 %collective-permute-start.7 = (bf16[128,2560]{1,0:T(8,128)(2,1)S(1)}, bf16[128,2560]{1,0:T(8,128)(2,1)S(1)}, u32[]{:S(2)}, u32[]{:S(2)}) collective-permute-start(bf16[128,2560]{1,0:T(8,128)(2,1)S(1)} %fusion.19), channel_id=1, source_target_pairs={{0,1},{1,0},{2,3},{3,2},{4,5},{5,4},{6,7},{7,6},{8,9},{9,8},{10,11... | collective-permute-start | bytes 1966088 | tf_op jit(solution)/shard_map/ppermute | solution.py:247
  65.7 8.4 %collective-permute-start.12 = (bf16[128,768]{1,0:T(8,128)(2,1)S(1)}, bf16[128,768]{1,0:T(8,128)(2,1)S(1)}, u32[]{:S(2)}, u32[]{:S(2)}) collective-permute-start(bf16[128,768]{1,0:T(8,128)(2,1)S(1)} %add_convert_fusion.3), channel_id=1, source_target_pairs={{0,2},{1,3},{2,4},{3,5},{4,6},{5,7},{6,0},{7,1},{8,10},{9,11},{10,... | collective-permute-start | bytes 589832 | tf_op jit(solution)/shard_map/ppermute | solution.py:244
  65.9 8.2 %collective-permute-start.10 = (bf16[128,768]{1,0:T(8,128)(2,1)S(1)}, bf16[128,768]{1,0:T(8,128)(2,1)S(1)}, u32[]{:S(2)}, u32[]{:S(2)}) collective-permute-start(bf16[128,768]{1,0:T(8,128)(2,1)S(1)} %add_convert_fusion.4), channel_id=1, source_target_pairs={{0,6},{1,7},{2,0},{3,1},{4,2},{5,3},{6,4},{7,5},{8,14},{9,15},{10,... | collective-permute-start | bytes 589832 | tf_op jit(solution)/shard_map/ppermute | solution.py:244
  74.3 1.2 copy-start.2
  74.3 1.2 copy-start.3
  84.3 130.8 %copy-start.4 = (f32[128,4096]{1,0:T(8,128)}, f32[128,4096]{1,0:T(8,128)S(1)}, u32[]{:S(2)}) copy-start(f32[128,4096]{1,0:T(8,128)S(1)} %get-tuple-element.22.hidden_ref) | copy-start | bytes 6291460
  232.3 37.9 %all-to-all-start.2 = ((bf16[128,8,1024]{2,1,0:T(8,128)(2,1)}), bf16[128,8,1024]{2,1,0:T(8,128)(2,1)S(1)}, u32[]{:S(2)}, u32[]{:S(2)}) async-start(bf16[128,8,1024]{2,1,0:T(8,128)(2,1)} %bitcast.68), calls=%async_computation.2 | async-start | bytes 4194304 | tf_op jit(solution)/shard_map/all_to_all | solution.py:303
  239.7 2.8 copy-start
  242.5 2.8 copy-start.1
  270.2 10.2 %copy-start.9 = (f32[128,8]{0,1:T(8,128)S(1)}, f32[128,8]{0,1:T(8,128)}, u32[]{:S(2)}) copy-start(f32[128,8]{0,1:T(8,128)} %param.14) | copy-start | bytes 12292
  270.2 113.0 %all-to-all-start.1 = ((bf16[128,8,4096]{2,1,0:T(8,128)(2,1)}), bf16[128,8,4096]{2,1,0:T(8,128)(2,1)}, u32[]{:S(2)}, u32[]{:S(2)}) async-start(bf16[128,8,4096]{2,1,0:T(8,128)(2,1)} %bitcast.61), calls=%async_computation.1 | async-start | bytes 16777216 | tf_op jit(solution)/shard_map/all_to_all | solution.py:303
  383.3 1.6 copy-start.5

commit v2 on v1

--- a/solution.py
+++ b/solution.py
@@ -8,6 +8,7 @@
 F32, BF16 = jnp.float32, jnp.bfloat16
 MAIN = 8
 PIECES = 4
+LANES = 128
 VMEM = 40 * 2**20
 
 
@@ -32,14 +33,13 @@
     hi = prob.astype(BF16)
     lo = (prob - hi.astype(F32)).astype(BF16)
     both = jnp.concatenate([hi, lo], axis=1)
-    row = jnp.arange(MAIN, dtype=jnp.int32)
 
     def spread(names):
         hot = slot[:, None, :] == names[None, :, None]
         hot = jnp.concatenate([hot, hot], axis=2)
-        return jnp.where(hot, both[:, None, :], jnp.zeros((), BF16)).reshape(experts * MAIN, 2 * toks).T
-
-    return spread(row), spread(MAIN + row // PIECES)
+        return jnp.where(hot, both[:, None, :], jnp.zeros((), BF16)).reshape(experts * names.size, 2 * toks).T
+
+    return spread(jnp.arange(MAIN, dtype=jnp.int32)), spread(MAIN + jnp.arange(MAIN // PIECES, dtype=jnp.int32))
 
 
 def build(slot, near, far, residual, gain):
@@ -75,10 +75,8 @@
         @pl.when(step == PIECES)
         def _():
             spill = slots == MAIN + row // PIECES
-            total = jnp.zeros((flat, tile), F32)
-            for c in range(PIECES):
-                total = total + dot(hot(spill & (row % PIECES == c)), normed[c])
-            out_ref[...] = total.astype(BF16)
+            parts = [hot(spill & (row % PIECES == c)) for c in range(PIECES)]
+            out_ref[...] = dot(jnp.concatenate(parts, axis=1), normed[...].reshape(PIECES * toks, tile)).astype(BF16)
 
     whole = lambda i: (0, 0)
     return pl.pallas_call(
@@ -107,78 +105,30 @@
     return (gate * jax.nn.sigmoid(gate) * up).astype(BF16)
 
 
-def spill_expert(got, w_gate, w_up, w_down):
+def expert(got, w_gate, w_up, w_down, block=256):
     flat, columns = got.shape
-    hid = w_gate.shape[1]
-    tile = columns // (PIECES + 1)
-    rows = flat // PIECES
-
-    def picks(c, shape, out_dim):
-        out = lax.broadcasted_iota(jnp.int32, shape, out_dim)
-        source = lax.broadcasted_iota(jnp.int32, shape, 1 - out_dim)
-        return jnp.where(source == out * PIECES + c, 1.0, 0.0).astype(BF16)
-
-    def kernel(got_ref, gate_ref, up_ref, down_ref, out_ref, gate_sum, up_sum, active, total):
-        step = pl.program_id(0)
-
-        @pl.when(step == 0)
-        def _():
-            gate_sum[...] = jnp.zeros_like(gate_sum)
-            up_sum[...] = jnp.zeros_like(up_sum)
-            total[...] = jnp.zeros_like(total)
-
-        @pl.when(step < PIECES)
-        def _():
-            value = dot(picks(step, (rows, flat), 0), got_ref[...]).astype(BF16)
-            gate_sum[...] += dot(value, gate_ref[...])
-            up_sum[...] += dot(value, up_ref[...])
-
-        @pl.when(step == PIECES)
-        def _():
-            active[...] = silu_times(gate_sum[...], up_sum[...])
-
-        @pl.when(step >= PIECES)
-        def _():
-            value = dot(active[...], down_ref[...]).astype(BF16)
-            total[...] += dot(picks(step - PIECES, (flat, rows), 1), value)
-
-        @pl.when(step == 2 * PIECES - 1)
-        def _():
-            out_ref[...] = total[...].astype(BF16)
-
-    early = lambda i: (jnp.minimum(i, PIECES - 1), 0)
-    return pl.pallas_call(
-        kernel,
-        grid=(2 * PIECES,),
-        in_specs=[
-            pl.BlockSpec((flat, tile), lambda i: (0, PIECES)),
-            pl.BlockSpec((tile, hid), early),
-            pl.BlockSpec((tile, hid), early),
-            pl.BlockSpec((hid, tile), lambda i: (0, jnp.maximum(i - PIECES, 0))),
-        ],
-        out_specs=pl.BlockSpec((flat, tile), lambda i: (0, 0)),
-        out_shape=jax.ShapeDtypeStruct((flat, tile), BF16),
-        scratch_shapes=[
-            pltpu.VMEM((rows, hid), F32),
-            pltpu.VMEM((rows, hid), F32),
-            pltpu.VMEM((rows, hid), BF16),
-            pltpu.VMEM((flat, tile), F32),
-        ],
-        compiler_params=pltpu.CompilerParams(vmem_limit_bytes=63 * 2**20),
-        cost_estimate=pl.CostEstimate(flops=9 * 10**9, bytes_accessed=23 * 10**6, transcendentals=0),
-        name="spill_expert",
-    )(got, w_gate, w_up, w_down)
-
-
-def main_expert(got, w_gate, w_up, w_down):
     width, hid = w_gate.shape
-    flat = got.shape[0]
-    block = 256
-
-    def kernel(rows_ref, gate_ref, up_ref, down_ref, out_ref):
-        rows = rows_ref[...]
-        active = silu_times(dot(rows, gate_ref[...]), dot(rows, up_ref[...]))
-        out_ref[...] = dot(active, down_ref[...]).astype(BF16)
+    tile = columns - width
+    extra = block // PIECES
+
+    def kernel(got_ref, gate_ref, up_ref, down_ref, out_ref, rows, spill):
+        rows[:block] = got_ref[:, :width]
+        for c in range(tile // LANES):
+            spill[c] = got_ref[:, width + c * LANES : width + (c + 1) * LANES].astype(F32)
+        for c in range(PIECES):
+            for d in range(tile // LANES):
+                at = c * tile + d * LANES
+                rows[block:, at : at + LANES] = spill[d, pl.ds(c, extra, stride=PIECES), :].astype(BF16)
+        value = rows[...]
+        active = silu_times(dot(value, gate_ref[...]), dot(value, up_ref[...]))
+        for c in range(PIECES):
+            cols = slice(c * tile, (c + 1) * tile)
+            made = dot(active, down_ref[:, cols])
+            out_ref[:, cols] = made[:block].astype(BF16)
+            for d in range(tile // LANES):
+                spill[d, pl.ds(c, extra, stride=PIECES), :] = made[block:, d * LANES : (d + 1) * LANES]
+        for d in range(tile // LANES):
+            out_ref[:, width + d * LANES : width + (d + 1) * LANES] = spill[d].astype(BF16)
 
     whole = lambda i: (0, 0)
     once = pl.Buffered(1)
@@ -186,51 +136,68 @@
         kernel,
         grid=(flat // block,),
         in_specs=[
-            pl.BlockSpec((block, width), lambda i: (i, 0)),
+            pl.BlockSpec((block, columns), lambda i: (i, 0)),
             pl.BlockSpec((width, hid), whole, pipeline_mode=once),
             pl.BlockSpec((width, hid), whole, pipeline_mode=once),
             pl.BlockSpec((hid, width), whole, pipeline_mode=once),
         ],
-        out_specs=pl.BlockSpec((block, width), lambda i: (i, 0)),
-        out_shape=jax.ShapeDtypeStruct((flat, width), BF16),
+        out_specs=pl.BlockSpec((block, columns), lambda i: (i, 0)),
+        out_shape=jax.ShapeDtypeStruct((flat, columns), BF16),
+        scratch_shapes=[
+            pltpu.VMEM((block + extra, width), BF16),
+            pltpu.VMEM((tile // LANES, block, LANES), F32),
+        ],
         compiler_params=pltpu.CompilerParams(vmem_limit_bytes=VMEM),
-        cost_estimate=pl.CostEstimate(flops=20 * 10**9, bytes_accessed=36 * 10**6, transcendentals=10**6),
-        name="main_expert",
+        cost_estimate=pl.CostEstimate(flops=24 * 10**9, bytes_accessed=40 * 10**6, transcendentals=10**6),
+        name="expert_rows",
     )(got, w_gate, w_up, w_down)
 
 
-def combine(main_w, spill_w, main_rows, spill_rows, hidden):
+def combine(main_w, spill_w, back, hidden):
     toks, width = hidden.shape
-    flat = main_rows.shape[0]
-    quarter = spill_rows.shape[1]
+    flat = back.shape[0]
     halves = 2
-    tile = quarter // halves
-
-    def kernel(main_w_ref, spill_w_ref, main_ref, spill_ref, hidden_ref, out_ref):
-        piece = pl.program_id(0) // halves
-        column = lax.broadcasted_iota(jnp.int32, (2 * toks, flat), 1)
-        spill = jnp.where(column % PIECES == piece, spill_w_ref[...].astype(F32), 0.0).astype(BF16)
-        both = dot(main_w_ref[...], main_ref[...]) + dot(spill, spill_ref[...])
+    tile = (back.shape[1] - width) // halves
+    tiles = width // tile
+
+    few = flat // PIECES
+
+    def kernel(main_w_ref, spill_w_ref, main_ref, spill_ref, hidden_ref, out_ref, spill, rows):
+        piece = pl.program_id(1)
+
+        @pl.when(piece == 0)
+        def _():
+            for d in range(tile // LANES):
+                spill[d] = spill_ref[:, d * LANES : (d + 1) * LANES].astype(F32)
+            for c in range(PIECES):
+                for d in range(tile // LANES):
+                    picked = spill[d, pl.ds(c, few, stride=PIECES), :]
+                    rows[c, :, d * LANES : (d + 1) * LANES] = picked.astype(BF16)
+
+        both = dot(main_w_ref[...], main_ref[...]) + dot(spill_w_ref[...], rows[piece])
         out_ref[...] = (hidden_ref[...] + (both[:toks] + both[toks:])).astype(BF16)
 
-    whole = lambda i: (0, 0)
-    along = lambda i: (0, i)
+    along = lambda half, piece: (0, piece * halves + half)
     return pl.pallas_call(
         kernel,
-        grid=(PIECES * halves,),
+        grid=(halves, PIECES),
         in_specs=[
-            pl.BlockSpec((2 * toks, flat), whole),
-            pl.BlockSpec((2 * toks, flat), whole),
+            pl.BlockSpec((2 * toks, flat), lambda half, piece: (0, 0)),
+            pl.BlockSpec((2 * toks, few), lambda half, piece: (0, 0)),
             pl.BlockSpec((flat, tile), along),
-            pl.BlockSpec((flat, tile), lambda i: (0, i % halves)),
+            pl.BlockSpec((flat, tile), lambda half, piece: (0, tiles + half)),
             pl.BlockSpec((toks, tile), along),
         ],
         out_specs=pl.BlockSpec((toks, tile), along),
         out_shape=jax.ShapeDtypeStruct((toks, width), BF16),
-        compiler_params=pltpu.CompilerParams(vmem_limit_bytes=VMEM),
+        scratch_shapes=[
+            pltpu.VMEM((tile // LANES, flat, LANES), F32),
+            pltpu.VMEM((PIECES, few, tile), BF16),
+        ],
+        compiler_params=pltpu.CompilerParams(vmem_limit_bytes=63 * 2**20),
         cost_estimate=pl.CostEstimate(flops=4 * 10**9, bytes_accessed=15 * 10**6, transcendentals=0),
         name="combine_rows",
-    )(main_w, spill_w, main_rows, spill_rows, hidden)
+    )(main_w, spill_w, back, back, hidden)
 
 
 def project_scatter(attn_heads, out_weight, toks):
@@ -303,13 +270,8 @@
         v = lax.all_to_all(v.reshape(experts, MAIN, cols), ("dp", "tensor"), split_axis=0, concat_axis=0, tiled=True)
         return v.reshape(flat, cols)
 
-    got = swap(sent)
-    w = (expert_gate[0], expert_up[0], expert_down[0])
-    spill_out = spill_expert(got, *w)
-    spill_out, got = lax.optimization_barrier((spill_out, got))
-    spill_back = swap(spill_out)
-    main_back = swap(main_expert(got, *w))
-    return combine(main_w, spill_w, main_back, spill_back, hidden)
+    made = expert(swap(sent), expert_gate[0], expert_up[0], expert_down[0])
+    return combine(main_w, spill_w, swap(made), hidden)
 
 
 def solution(mesh):

time: 398 us -> 397 us (level)
  waiting for transfers between devices: 137 us -> 165 us
  Pallas kernels: 60.6 us -> 48.7 us
  starting transfers between devices: 41 us -> 31.2 us
  local copies, waits for them, and re-layouts: 11.3 us -> 3.84 us
    all_to_all x2 -> x1, waiting for transfers between devices: 99.8 us -> 128 us  [swap(): lax.all_to_all(v.reshape(experts, MAIN, cols), ('dp', 'tensor'), split_ax...]
    pallas_call x3 -> x2, Pallas kernels: 51.8 us -> 40.9 us  [the longest x1 30.6 us: expert(): pl.pallas_call(kernel, grid=(flat // block,), in_specs=[pl.BlockSpec((blo...]
    all_to_all x2 -> x1, starting transfers between devices: 17.6 us -> 7.8 us  [swap(): lax.all_to_all(v.reshape(experts, MAIN, cols), ('dp', 'tensor'), split_ax...]
    unnamed x20 -> x22, local copies, waits for them, and re-layouts: 8.24 us -> 1.11 us
  transfers between devices with their start and end apart: 16 -> 15, of which waited for: 9 -> 9; matrix products, arithmetic and copies ran while one was open for 2% -> 2% of each run, Pallas kernels for 6% -> 0%
where the time goes in v2:
time: 397 us; the launch traced here: 393 us
  waiting for transfers between devices  165 us (42%)
  blocking collectives  131 us (33%)
  Pallas kernels  48.7 us (12%)
  starting transfers between devices  31.2 us (8%)
  matrix products  10.5 us (3%)
    all_to_all x1, blocking collectives, swap(): lax.all_to_all(v.reshape(experts, MAIN, cols), ('dp', 'tensor'), split_ax...  131 us
    all_to_all x1, waiting for transfers between devices, swap(): lax.all_to_all(v.reshape(experts, MAIN, cols), ('dp', 'tensor'), split_ax...  128 us
    ppermute x12, waiting for transfers between devices, along_x(): lax.ppermute(v, 'tensor', [(i * 2 + j, (i + by) % 4 * 2 + j) for i in ran...  37.1 us
    pallas_call x1, Pallas kernels, expert(): pl.pallas_call(kernel, grid=(flat // block,), in_specs=[pl.BlockSpec((blo...  30.6 us
    ppermute x12, starting transfers between devices, along_x(): lax.ppermute(v, 'tensor', [(i * 2 + j, (i + by) % 4 * 2 + j) for i in ran...  18.2 us
    dot_general x11, matrix products, dot(): return jnp.dot(a, b, preferred_element_type=F32)  10.5 us
    pallas_call x1, Pallas kernels, combine(): pl.pallas_call(kernel, grid=(halves, PIECES), in_specs=[pl.BlockSpec((2 *...  10.3 us
  transfers between devices with their start and end apart: 15, of which 9 were waited for; matrix products, arithmetic and copies ran while one was open for 2% of the time, Pallas kernels for 0%

profile of v2, /device:TPU:1, one launch (start us, length us, event | category | flops | bytes accessed | tf_op | source)
XLA Modules:
  0.0 393.4 jit_solution(6848773762031245981)
XLA Ops:
  0.0 1.3 constant_dynamic-slice_fusion.1
  1.3 1.8 convolution_convert_fusion.8
  3.1 1.9 convolution_convert_fusion.9
  5.2 2.5 convolution_convert_fusion
  7.7 4.5 %collective-permute-start = (bf16[512,1536]{1,0:T(8,128)(2,1)S(1)}, bf16[512,1536]{1,0:T(8,128)(2,1)S(1)}, u32[]{:S(2)}, u32[]{:S(2)}) collective-permute-start(bf16[512,1536]{1,0:T(8,128)(2,1)S(1)} %convolution_convert_fusion), channel_id=1, source_target_pairs={{0,1},{1,0},{2,3},{3,2},{4,5},{5,4},{6,7},{7,6},{8,9},{9,8},{10,11... | collective-permute-start | bytes 4718600 | tf_op jit(solution)/shard_map/ppermute | solution.py:214
  12.2 2.5 collective-permute-start.2
  14.7 0.5 convolution_convert_fusion.6
  15.3 0.2 collective-permute-start.4
  15.5 0.5 convolution_convert_fusion.2
  16.0 2.6 collective-permute-start.6
  18.7 9.1 %collective-permute-done.2 = bf16[256,1280]{1,0:T(8,128)(2,1)S(1)} collective-permute-done((bf16[256,1280]{1,0:T(8,128)(2,1)S(1)}, bf16[256,1280]{1,0:T(8,128)(2,1)S(1)}, u32[]{:S(2)}, u32[]{:S(2)}) %collective-permute-start.2) | collective-permute-done | bytes 655392 | tf_op jit(solution)/shard_map/ppermute | solution.py:211
  27.8 0.5 add_convert_fusion.2
  28.3 3.5 collective-permute-start.3
  31.8 13.8 %collective-permute-done.4 = bf16[256,1280]{1,0:T(8,128)(2,1)S(1)} collective-permute-done((bf16[256,1280]{1,0:T(8,128)(2,1)S(1)}, bf16[256,1280]{1,0:T(8,128)(2,1)S(1)}, u32[]{:S(2)}, u32[]{:S(2)}) %collective-permute-start.4) | collective-permute-done | bytes 655392 | tf_op jit(solution)/shard_map/ppermute | solution.py:211
  45.6 0.5 add_convert_fusion.1
  46.2 0.2 collective-permute-done
  46.4 1.0 add_convert_fusion
  47.4 0.5 fusion
  47.9 0.1 dynamic-slice_bitcast_fusion.3
  48.0 0.5 fusion.2
  48.6 1.3 collective-permute-start.11
  49.9 1.5 collective-permute-start.9
  51.5 4.4 %collective-permute-done.3 = bf16[256,1280]{1,0:T(8,128)(2,1)S(1)} collective-permute-done((bf16[256,1280]{1,0:T(8,128)(2,1)S(1)}, bf16[256,1280]{1,0:T(8,128)(2,1)S(1)}, u32[]{:S(2)}, u32[]{:S(2)}) %collective-permute-start.3) | collective-permute-done | bytes 655392 | tf_op jit(solution)/shard_map/ppermute | solution.py:211
  55.9 3.4 collective-permute-start.13
  59.3 0.2 convert_add_fusion.1
  59.6 1.8 collective-permute-done.5
  61.4 0.2 convert_add_fusion
  61.7 0.3 pad_maximum_fusion
  62.1 0.7 collective-permute-start.7
  62.8 2.8 collective-permute-done.11
  65.9 2.9 collective-permute-start.10
  68.8 0.1 fusion.6.slot_ref
  68.9 0.9 collective-permute-done.8
  69.9 4.2 %collective-permute-done.12 = bf16[128,768]{1,0:T(8,128)(2,1)S(1)} collective-permute-done((bf16[128,768]{1,0:T(8,128)(2,1)S(1)}, bf16[128,768]{1,0:T(8,128)(2,1)S(1)}, u32[]{:S(2)}, u32[]{:S(2)}) %collective-permute-start.12) | collective-permute-done | bytes 196640 | tf_op jit(solution)/shard_map/ppermute | solution.py:211
  74.1 0.1 convert_add_fusion.3
  74.3 0.1 bitcast_add_fusion.near_ref
  74.5 1.1 copy-done.1
  75.5 7.8 %build_rows.1 = (bf16[1024,5120]{1,0:T(8,128)(2,1)}, f32[128,4096]{1,0:T(8,128)S(1)}) custom-call(s32[128,128]{1,0:T(8,128)S(1)} %fusion.6.slot_ref, f32[128,2560]{1,0:T(8,128)S(1)} %bitcast_add_fusion.near_ref, f32[128,1536]{1,0:T(8,128)S(1)} %pad_maximum_fusion.1.far_ref, bf16[128,4096]{1,0:T(8,128)(2,1)S(1)} %copy-done.1, f32[1,4096]{1,0:T(1,128)S(1)} %bitcast.57), custom_call_target="tpu_custom_call" | custom-call | flops 3000000000 | bytes 15000000 | tf_op jit(solution)/shard_map/build_rows/pallas_call | solution.py:82
  83.3 130.8 %all_to_all.10 = bf16[128,8,5120]{2,1,0:T(8,128)(2,1)} all-to-all(bf16[128,8,5120]{2,1,0:T(8,128)(2,1)} %bitcast.59), channel_id=1, replica_groups=mesh['dp'=16,'tensor'=8] {'dp','tensor'}, dimensions={0} | all-to-all | bytes 20971520 | tf_op jit(solution)/shard_map/all_to_all | solution.py:270
  214.2 30.6 %expert_rows.1 = bf16[1024,5120]{1,0:T(8,128)(2,1)} custom-call(bf16[1024,5120]{1,0:T(8,128)(2,1)} %bitcast.60, bf16[4096,768]{1,0:T(8,128)(2,1)S(1)} %bitcast.53, bf16[4096,768]{1,0:T(8,128)(2,1)S(1)} %bitcast.56, bf16[768,4096]{1,0:T(8,128)(2,1)} %bitcast.80), custom_call_target="tpu_custom_call" | custom-call | flops 24000000000 | bytes 40000000 | tf_op jit(solution)/shard_map/expert_rows/pallas_call | solution.py:135
  244.8 7.8 %all-to-all-start.1 = ((bf16[128,8,5120]{2,1,0:T(8,128)(2,1)}), bf16[128,8,5120]{2,1,0:T(8,128)(2,1)}, u32[]{:S(2)}, u32[]{:S(2)}) async-start(bf16[128,8,5120]{2,1,0:T(8,128)(2,1)} %bitcast.58), calls=%async_computation.1 | async-start | bytes 20971520 | tf_op jit(solution)/shard_map/all_to_all | solution.py:270
  252.8 0.2 copy.17
  253.1 0.2 copy.16
  253.8 0.1 eq.75
  254.0 0.7 fusion.22.spill_w_ref
  254.7 0.9 fusion.20.main_w_ref
  255.6 127.5 %all-to-all-done.1 = bf16[128,8,5120]{2,1,0:T(8,128)(2,1)} async-done(((bf16[128,8,5120]{2,1,0:T(8,128)(2,1)}), bf16[128,8,5120]{2,1,0:T(8,128)(2,1)}, u32[]{:S(2)}, u32[]{:S(2)}) %all-to-all-start.1) | async-done | bytes 10485792 | tf_op jit(solution)/shard_map/all_to_all | solution.py:270
  383.1 10.3 %combine_rows.1 = bf16[128,4096]{1,0:T(8,128)(2,1)} custom-call(bf16[256,1024]{1,0:T(8,128)(2,1)} %fusion.20.main_w_ref, bf16[256,256]{1,0:T(8,128)(2,1)} %fusion.22.spill_w_ref, bf16[1024,5120]{1,0:T(8,128)(2,1)} %bitcast.29.main_ref.spill_ref, bf16[1024,5120]{1,0:T(8,128)(2,1)} %bitcast.29.main_ref.spill_ref, f32[128,4096]{1,0:T(8,128)} %copy-done), custom_call_target="tpu_custom_call" | custom-call | flops 4000000000 | bytes 15000000 | tf_op jit(solution)/shard_map/combine_rows/pallas_call | solution.py:181
  (58 shorter events, 1.6 us)
Async XLA Ops:
  3.1 2.0 copy-start.3
  5.2 9.6 %copy-start.4 = (bf16[512,4096]{1,0:T(8,128)(2,1)S(1)}, bf16[512,4096]{1,0:T(8,128)(2,1)}, u32[]{:S(2)}) copy-start(bf16[512,4096]{1,0:T(8,128)(2,1)} %param.10) | copy-start | bytes 12582916
  7.7 38.6 %collective-permute-start = (bf16[512,1536]{1,0:T(8,128)(2,1)S(1)}, bf16[512,1536]{1,0:T(8,128)(2,1)S(1)}, u32[]{:S(2)}, u32[]{:S(2)}) collective-permute-start(bf16[512,1536]{1,0:T(8,128)(2,1)S(1)} %convolution_convert_fusion), channel_id=1, source_target_pairs={{0,1},{1,0},{2,3},{3,2},{4,5},{5,4},{6,7},{7,6},{8,9},{9,8},{10,11... | collective-permute-start | bytes 4718600 | tf_op jit(solution)/shard_map/ppermute | solution.py:214
  12.2 15.6 %collective-permute-start.2 = (bf16[256,1280]{1,0:T(8,128)(2,1)S(1)}, bf16[256,1280]{1,0:T(8,128)(2,1)S(1)}, u32[]{:S(2)}, u32[]{:S(2)}) collective-permute-start(bf16[256,1280]{1,0:T(8,128)(2,1)S(1)} %convolution_convert_fusion.8), channel_id=1, source_target_pairs={{0,6},{1,7},{2,0},{3,1},{4,2},{5,3},{6,4},{7,5},{8,14},{9,15},{10,... | collective-permute-start | bytes 1966088 | tf_op jit(solution)/shard_map/ppermute | solution.py:211
  15.2 3.4 copy-start.5
  15.3 34.7 %collective-permute-start.1 = (bf16[256,1280]{1,0:T(8,128)(2,1)S(1)}, bf16[256,1280]{1,0:T(8,128)(2,1)S(1)}, u32[]{:S(2)}, u32[]{:S(2)}) collective-permute-start(bf16[256,1280]{1,0:T(8,128)(2,1)S(1)} %convolution_convert_fusion.6), channel_id=1, source_target_pairs={{0,2},{1,3},{2,4},{3,5},{4,6},{5,7},{6,0},{7,1},{8,10},{9,11},{10,... | collective-permute-start | bytes 1966088 | tf_op jit(solution)/shard_map/ppermute | solution.py:211
  15.3 30.2 %collective-permute-start.4 = (bf16[256,1280]{1,0:T(8,128)(2,1)S(1)}, bf16[256,1280]{1,0:T(8,128)(2,1)S(1)}, u32[]{:S(2)}, u32[]{:S(2)}) collective-permute-start(bf16[256,1280]{1,0:T(8,128)(2,1)S(1)} %convolution_convert_fusion.9), channel_id=1, source_target_pairs={{0,2},{1,3},{2,4},{3,5},{4,6},{5,7},{6,0},{7,1},{8,10},{9,11},{10,... | collective-permute-start | bytes 1966088 | tf_op jit(solution)/shard_map/ppermute | solution.py:211
  16.0 43.5 %collective-permute-start.6 = (bf16[256,1280]{1,0:T(8,128)(2,1)S(1)}, bf16[256,1280]{1,0:T(8,128)(2,1)S(1)}, u32[]{:S(2)}, u32[]{:S(2)}) collective-permute-start(bf16[256,1280]{1,0:T(8,128)(2,1)S(1)} %convolution_convert_fusion.2), channel_id=1, source_target_pairs={{0,6},{1,7},{2,0},{3,1},{4,2},{5,3},{6,4},{7,5},{8,14},{9,15},{10,... | collective-permute-start | bytes 1966088 | tf_op jit(solution)/shard_map/ppermute | solution.py:211
  28.3 27.6 %collective-permute-start.3 = (bf16[256,1280]{1,0:T(8,128)(2,1)S(1)}, bf16[256,1280]{1,0:T(8,128)(2,1)S(1)}, u32[]{:S(2)}, u32[]{:S(2)}) collective-permute-start(bf16[256,1280]{1,0:T(8,128)(2,1)S(1)} %add_convert_fusion.2), channel_id=1, source_target_pairs={{0,6},{1,7},{2,0},{3,1},{4,2},{5,3},{6,4},{7,5},{8,14},{9,15},{10,... | collective-permute-start | bytes 1966088 | tf_op jit(solution)/shard_map/ppermute | solution.py:211
  46.1 15.3 %collective-permute-start.5 = (bf16[256,1280]{1,0:T(8,128)(2,1)S(1)}, bf16[256,1280]{1,0:T(8,128)(2,1)S(1)}, u32[]{:S(2)}, u32[]{:S(2)}) collective-permute-start(bf16[256,1280]{1,0:T(8,128)(2,1)S(1)} %add_convert_fusion.1), channel_id=1, source_target_pairs={{0,2},{1,3},{2,4},{3,5},{4,6},{5,7},{6,0},{7,1},{8,10},{9,11},{10,... | collective-permute-start | bytes 1966088 | tf_op jit(solution)/shard_map/ppermute | solution.py:211
  48.6 17.1 %collective-permute-start.11 = (bf16[128,768]{1,0:T(8,128)(2,1)S(1)}, bf16[128,768]{1,0:T(8,128)(2,1)S(1)}, u32[]{:S(2)}, u32[]{:S(2)}) collective-permute-start(bf16[128,768]{1,0:T(8,128)(2,1)S(1)} %get-tuple-element.34), channel_id=1, source_target_pairs={{0,2},{1,3},{2,4},{3,5},{4,6},{5,7},{6,0},{7,1},{8,10},{9,11},{10,... | collective-permute-start | bytes 589832 | tf_op jit(solution)/shard_map/ppermute | solution.py:211
  49.9 15.9 %collective-permute-start.9 = (bf16[128,768]{1,0:T(8,128)(2,1)S(1)}, bf16[128,768]{1,0:T(8,128)(2,1)S(1)}, u32[]{:S(2)}, u32[]{:S(2)}) collective-permute-start(bf16[128,768]{1,0:T(8,128)(2,1)S(1)} %get-tuple-element.33), channel_id=1, source_target_pairs={{0,6},{1,7},{2,0},{3,1},{4,2},{5,3},{6,4},{7,5},{8,14},{9,15},{10,... | collective-permute-start | bytes 589832 | tf_op jit(solution)/shard_map/ppermute | solution.py:211
  55.9 13.0 %collective-permute-start.13 = (bf16[128,768]{1,0:T(8,128)(2,1)S(1)}, bf16[128,768]{1,0:T(8,128)(2,1)S(1)}, u32[]{:S(2)}, u32[]{:S(2)}) collective-permute-start(bf16[128,768]{1,0:T(8,128)(2,1)S(1)} %slice.58), channel_id=1, source_target_pairs={{0,6},{1,7},{2,0},{3,1},{4,2},{5,3},{6,4},{7,5},{8,14},{9,15},{10,... | collective-permute-start | bytes 589832 | tf_op jit(solution)/shard_map/ppermute | solution.py:211
  59.5 10.3 %collective-permute-start.8 = (bf16[128,768]{1,0:T(8,128)(2,1)S(1)}, bf16[128,768]{1,0:T(8,128)(2,1)S(1)}, u32[]{:S(2)}, u32[]{:S(2)}) collective-permute-start(bf16[128,768]{1,0:T(8,128)(2,1)S(1)} %slice.52), channel_id=1, source_target_pairs={{0,2},{1,3},{2,4},{3,5},{4,6},{5,7},{6,0},{7,1},{8,10},{9,11},{10,... | collective-permute-start | bytes 589832 | tf_op jit(solution)/shard_map/ppermute | solution.py:211
  62.1 12.2 %collective-permute-start.7 = (bf16[128,2560]{1,0:T(8,128)(2,1)S(1)}, bf16[128,2560]{1,0:T(8,128)(2,1)S(1)}, u32[]{:S(2)}, u32[]{:S(2)}) collective-permute-start(bf16[128,2560]{1,0:T(8,128)(2,1)S(1)} %fusion.19), channel_id=1, source_target_pairs={{0,1},{1,0},{2,3},{3,2},{4,5},{5,4},{6,7},{7,6},{8,9},{9,8},{10,11... | collective-permute-start | bytes 1966088 | tf_op jit(solution)/shard_map/ppermute | solution.py:214
  65.7 8.4 %collective-permute-start.12 = (bf16[128,768]{1,0:T(8,128)(2,1)S(1)}, bf16[128,768]{1,0:T(8,128)(2,1)S(1)}, u32[]{:S(2)}, u32[]{:S(2)}) collective-permute-start(bf16[128,768]{1,0:T(8,128)(2,1)S(1)} %add_convert_fusion.3), channel_id=1, source_target_pairs={{0,2},{1,3},{2,4},{3,5},{4,6},{5,7},{6,0},{7,1},{8,10},{9,11},{10,... | collective-permute-start | bytes 589832 | tf_op jit(solution)/shard_map/ppermute | solution.py:211
  65.9 8.2 %collective-permute-start.10 = (bf16[128,768]{1,0:T(8,128)(2,1)S(1)}, bf16[128,768]{1,0:T(8,128)(2,1)S(1)}, u32[]{:S(2)}, u32[]{:S(2)}) collective-permute-start(bf16[128,768]{1,0:T(8,128)(2,1)S(1)} %add_convert_fusion.4), channel_id=1, source_target_pairs={{0,6},{1,7},{2,0},{3,1},{4,2},{5,3},{6,4},{7,5},{8,14},{9,15},{10,... | collective-permute-start | bytes 589832 | tf_op jit(solution)/shard_map/ppermute | solution.py:211
  74.3 1.2 copy-start.1
  74.3 1.2 copy-start.2
  75.5 138.6 %slice-start = ((s8[6291456]{0:T(1024)(128)(4,1)}), s8[4194304]{0:T(1024)(128)(4,1)S(1)}, s32[]{:S(2)}) async-start(s8[6291456]{0:T(1024)(128)(4,1)} %bitcast.51), calls=%async_computation.2 | async-start | bytes 8388608
  75.5 138.6 %slice-start.2 = ((s8[6291456]{0:T(1024)(128)(4,1)}), s8[4194304]{0:T(1024)(128)(4,1)S(1)}, s32[]{:S(2)}) async-start(s8[6291456]{0:T(1024)(128)(4,1)} %bitcast.54), calls=%async_computation.4 | async-start | bytes 8388608
  83.3 130.8 %copy-start = (f32[128,4096]{1,0:T(8,128)}, f32[128,4096]{1,0:T(8,128)S(1)}, u32[]{:S(2)}) copy-start(f32[128,4096]{1,0:T(8,128)S(1)} %get-tuple-element.18.hidden_ref) | copy-start | bytes 6291460
  83.3 130.8 %slice-start.1 = ((s8[6291456]{0:T(1024)(128)(4,1)}), s8[2097152]{0:T(1024)(128)(4,1)S(1)}, s32[]{:S(2)}) async-start(s8[6291456]{0:T(1024)(128)(4,1)} %bitcast.51), calls=%async_computation.3 | async-start | bytes 4194304
  83.3 130.8 %slice-start.3 = ((s8[6291456]{0:T(1024)(128)(4,1)}), s8[2097152]{0:T(1024)(128)(4,1)S(1)}, s32[]{:S(2)}) async-start(s8[6291456]{0:T(1024)(128)(4,1)} %bitcast.54), calls=%async_computation.5 | async-start | bytes 4194304
  244.8 7.8 %copy-start.6 = (f32[128,8]{0,1:T(8,128)S(1)}, f32[128,8]{0,1:T(8,128)}, u32[]{:S(2)}) copy-start(f32[128,8]{0,1:T(8,128)} %param.14) | copy-start | bytes 12292
  244.8 138.3 %all-to-all-start.1 = ((bf16[128,8,5120]{2,1,0:T(8,128)(2,1)}), bf16[128,8,5120]{2,1,0:T(8,128)(2,1)}, u32[]{:S(2)}, u32[]{:S(2)}) async-start(bf16[128,8,5120]{2,1,0:T(8,128)(2,1)} %bitcast.58), calls=%async_computation.1 | async-start | bytes 20971520 | tf_op jit(solution)/shard_map/all_to_all | solution.py:270

commit v3 on v2

--- a/solution.py
+++ b/solution.py
@@ -147,7 +147,7 @@
             pltpu.VMEM((block + extra, width), BF16),
             pltpu.VMEM((tile // LANES, block, LANES), F32),
         ],
-        compiler_params=pltpu.CompilerParams(vmem_limit_bytes=VMEM),
+        compiler_params=pltpu.CompilerParams(vmem_limit_bytes=30 * 2**20),
         cost_estimate=pl.CostEstimate(flops=24 * 10**9, bytes_accessed=40 * 10**6, transcendentals=10**6),
         name="expert_rows",
     )(got, w_gate, w_up, w_down)
@@ -194,7 +194,7 @@
             pltpu.VMEM((tile // LANES, flat, LANES), F32),
             pltpu.VMEM((PIECES, few, tile), BF16),
         ],
-        compiler_params=pltpu.CompilerParams(vmem_limit_bytes=63 * 2**20),
+        compiler_params=pltpu.CompilerParams(vmem_limit_bytes=16 * 2**20),
         cost_estimate=pl.CostEstimate(flops=4 * 10**9, bytes_accessed=15 * 10**6, transcendentals=0),
         name="combine_rows",
     )(main_w, spill_w, back, back, hidden)
@@ -263,6 +263,7 @@
     slot, prob = route(expert_ids, gate_probs, experts)
     main_w, spill_w = combine_weights(slot, prob)
     near, far = project_scatter(attn_heads, out_weight, toks)
+    near, main_w, spill_w = lax.optimization_barrier((near, main_w, spill_w))
     sent, hidden = build(slot, near, far, residual, norm_gain[None, :])
 
     def swap(v):

time: 397 us -> 383 us (0.965)
  waiting for transfers between devices: 165 us -> 32.8 us
  blocking collectives: 131 us -> 258 us
  matrix products: 10.5 us -> 21.8 us
  starting transfers between devices: 31.2 us -> 21.2 us
  Pallas kernels: 48.7 us -> 43 us
    all_to_all x1 -> x2, blocking collectives: 131 us -> 258 us  [swap(): lax.all_to_all(v.reshape(experts, MAIN, cols), ('dp', 'tensor'), split_ax...]
    all_to_all x1 -> x0, waiting for transfers between devices: 128 us -> none  [swap(): lax.all_to_all(v.reshape(experts, MAIN, cols), ('dp', 'tensor'), split_ax...]
    ppermute x12, waiting for transfers between devices: 37.1 us -> 19 us  [along_x(): lax.ppermute(v, 'tensor', [(i * 2 + j, (i + by) % 4 * 2 + j) for i in ran...]
    ppermute x2, waiting for transfers between devices: 0.18 us -> 13.8 us  [along_z(): return lax.ppermute(v, 'tensor', [(i, i ^ 1) for i in range(8)])]
    dot_general x11, matrix products: 10.5 us -> 21.8 us  [dot(): return jnp.dot(a, b, preferred_element_type=F32)]
    all_to_all x1 -> x0, starting transfers between devices: 7.8 us -> none  [swap(): lax.all_to_all(v.reshape(experts, MAIN, cols), ('dp', 'tensor'), split_ax...]
  transfers between devices with their start and end apart: 15 -> 14, of which waited for: 9 -> 6; matrix products, arithmetic and copies ran while one was open for 2% -> 6% of each run, Pallas kernels for 0% -> 0%
where the time goes in v3:
time: 383 us
  blocking collectives  258 us (67%)
  Pallas kernels  43 us (11%)
  waiting for transfers between devices  32.8 us (9%)
  matrix products  21.8 us (6%)
  starting transfers between devices  21.2 us (6%)
    all_to_all x2, blocking collectives, swap(): lax.all_to_all(v.reshape(experts, MAIN, cols), ('dp', 'tensor'), split_ax...  258 us
    pallas_call x1, Pallas kernels, expert(): pl.pallas_call(kernel, grid=(flat // block,), in_specs=[pl.BlockSpec((blo...  28.8 us
    dot_general x11, matrix products, dot(): return jnp.dot(a, b, preferred_element_type=F32)  21.8 us
    ppermute x12, waiting for transfers between devices, along_x(): lax.ppermute(v, 'tensor', [(i * 2 + j, (i + by) % 4 * 2 + j) for i in ran...  19 us
    ppermute x12, starting transfers between devices, along_x(): lax.ppermute(v, 'tensor', [(i * 2 + j, (i + by) % 4 * 2 + j) for i in ran...  14.6 us
    ppermute x2, waiting for transfers between devices, along_z(): return lax.ppermute(v, 'tensor', [(i, i ^ 1) for i in range(8)])  13.8 us
    pallas_call x1, Pallas kernels, build(): pl.pallas_call(kernel, grid=(PIECES + 1,), in_specs=[pl.BlockSpec(slot.sh...  7.75 us
  transfers between devices with their start and end apart: 14, of which 6 were waited for; matrix products, arithmetic and copies ran while one was open for 6% of the time, Pallas kernels for 0%

profile of v3, /device:TPU:1, one launch (start us, length us, event | category | flops | bytes accessed | tf_op | source)
XLA Modules:
  0.0 382.7 jit_solution(7765857789365365601)
XLA Ops:
  0.0 1.3 constant_dynamic-slice_fusion.1
  1.3 2.9 convolution_convert_fusion.6
  4.2 2.0 collective-permute-start.1
  6.2 2.7 convolution_convert_fusion.2
  8.9 1.3 collective-permute-start.6
  10.1 2.7 convolution_convert_fusion.8
  12.8 2.8 convolution_convert_fusion.9
  15.7 1.5 collective-permute-start.2
  17.2 3.6 convolution_convert_fusion
  20.8 3.8 collective-permute-start
  24.7 0.1 fusion.6.slot_ref
  25.0 0.1 eq.75
  25.1 0.1 eq.69
  25.3 0.1 copy.18
  25.4 0.2 copy.16
  25.7 0.6 broadcast_compare_fusion.1
  26.5 0.1 copy.19
  26.6 0.2 copy.17
  26.9 11.6 %collective-permute-done.2 = bf16[256,1280]{1,0:T(8,128)(2,1)} collective-permute-done((bf16[256,1280]{1,0:T(8,128)(2,1)}, bf16[256,1280]{1,0:T(8,128)(2,1)}, u32[]{:S(2)}, u32[]{:S(2)}) %collective-permute-start.2) | collective-permute-done | bytes 655392 | tf_op jit(solution)/shard_map/ppermute | solution.py:211
  38.5 2.1 add_convert_fusion.2
  40.6 2.4 collective-permute-start.3
  43.0 1.7 add_convert_fusion.1
  44.8 13.0 %collective-permute-done = bf16[512,1536]{1,0:T(8,128)(2,1)} collective-permute-done((bf16[512,1536]{1,0:T(8,128)(2,1)}, bf16[512,1536]{1,0:T(8,128)(2,1)}, u32[]{:S(2)}, u32[]{:S(2)}) %collective-permute-start) | collective-permute-done | bytes 1572896 | tf_op jit(solution)/shard_map/ppermute | solution.py:214
  57.8 2.4 add_convert_fusion
  60.2 0.1 dynamic-slice_bitcast_fusion.3
  60.3 0.1 collective-permute-start.8
  60.4 0.5 fusion.2
  61.0 0.5 fusion
  61.5 2.7 collective-permute-start.13
  64.3 1.3 collective-permute-start.9
  65.5 0.2 convert_add_fusion
  65.7 0.3 collective-permute-start.11
  66.0 0.2 convert_add_fusion.1
  66.2 0.3 pad_maximum_fusion
  66.6 2.8 collective-permute-start.7
  69.4 1.4 collective-permute-done.9
  70.8 2.9 collective-permute-start.10
  73.9 2.4 collective-permute-done.10
  76.3 3.5 collective-permute-done.12
  79.8 0.1 convert_add_fusion.3
  80.1 0.8 collective-permute-done.7
  80.9 0.1 bitcast_add_fusion.near_ref
  81.0 0.3 copy-done
  81.3 7.8 %build_rows.1 = (bf16[1024,5120]{1,0:T(8,128)(2,1)}, f32[128,4096]{1,0:T(8,128)S(1)}) custom-call(s32[128,128]{1,0:T(8,128)S(1)} %fusion.6.slot_ref, f32[128,2560]{1,0:T(8,128)S(1)} %bitcast_add_fusion.near_ref, f32[128,1536]{1,0:T(8,128)S(1)} %pad_maximum_fusion.1.far_ref, bf16[128,4096]{1,0:T(8,128)(2,1)S(1)} %copy-done, f32[1,4096]{1,0:T(1,128)S(1)} %bitcast.62), custom_call_target="tpu_custom_call" | custom-call | flops 3000000000 | bytes 15000000 | tf_op jit(solution)/shard_map/build_rows/pallas_call | solution.py:82
  89.0 132.1 %all_to_all.10 = bf16[128,8,5120]{2,1,0:T(8,128)(2,1)} all-to-all(bf16[128,8,5120]{2,1,0:T(8,128)(2,1)} %bitcast.63), channel_id=1, replica_groups=mesh['dp'=16,'tensor'=8] {'dp','tensor'}, dimensions={0} | all-to-all | bytes 20971520 | tf_op jit(solution)/shard_map/all_to_all | solution.py:271
  221.2 28.8 %expert_rows.1 = bf16[1024,5120]{1,0:T(8,128)(2,1)} custom-call(bf16[1024,5120]{1,0:T(8,128)(2,1)} %bitcast.64, bf16[4096,768]{1,0:T(8,128)(2,1)S(1)} %bitcast.55, bf16[4096,768]{1,0:T(8,128)(2,1)S(1)} %bitcast.58, bf16[768,4096]{1,0:T(8,128)(2,1)S(1)} %bitcast.61), custom_call_target="tpu_custom_call" | custom-call | flops 24000000000 | bytes 40000000 | tf_op jit(solution)/shard_map/expert_rows/pallas_call | solution.py:135
  250.0 126.3 %all_to_all.11 = bf16[128,8,5120]{2,1,0:T(8,128)(2,1)S(1)} all-to-all(bf16[128,8,5120]{2,1,0:T(8,128)(2,1)} %bitcast.65), channel_id=1, replica_groups=mesh['dp'=16,'tensor'=8] {'dp','tensor'}, dimensions={0} | all-to-all | bytes 20971520 | tf_op jit(solution)/shard_map/all_to_all | solution.py:271
  376.3 6.5 %combine_rows.1 = bf16[128,4096]{1,0:T(8,128)(2,1)} custom-call(bf16[256,1024]{1,0:T(8,128)(2,1)S(1)} %fusion.20.main_w_ref, bf16[256,256]{1,0:T(8,128)(2,1)S(1)} %fusion.22.spill_w_ref, bf16[1024,5120]{1,0:T(8,128)(2,1)S(1)} %bitcast.51, bf16[1024,5120]{1,0:T(8,128)(2,1)S(1)} %bitcast.52, f32[128,4096]{1,0:T(8,128)S(1)} %get-tuple-element.24.hidden_ref), custom_call_target="tpu_custom_call" | custom-call | flops 4000000000 | bytes 15000000 | tf_op jit(solution)/shard_map/combine_rows/pallas_call | solution.py:181
  (66 shorter events, 1.2 us)
Async XLA Ops:
  1.3 4.9 %copy-start.4 = (bf16[1,2,128,512]{3,2,1,0:T(8,128)(2,1)}, bf16[1,2,128,512]{3,2,1,0:T(8,128)(2,1)S(1)}, u32[]{:S(2)}) copy-start(bf16[1,2,128,512]{3,2,1,0:T(8,128)(2,1)S(1)} %get-tuple-element.31) | copy-start | bytes 786436
  1.3 8.8 %copy-start.5 = (bf16[1,2,128,512]{3,2,1,0:T(8,128)(2,1)}, bf16[1,2,128,512]{3,2,1,0:T(8,128)(2,1)S(1)}, u32[]{:S(2)}) copy-start(bf16[1,2,128,512]{3,2,1,0:T(8,128)(2,1)S(1)} %get-tuple-element.32) | copy-start | bytes 786436
  4.2 61.6 %collective-permute-start.1 = (bf16[256,1280]{1,0:T(8,128)(2,1)}, bf16[256,1280]{1,0:T(8,128)(2,1)S(1)}, u32[]{:S(2)}, u32[]{:S(2)}) collective-permute-start(bf16[256,1280]{1,0:T(8,128)(2,1)} %convolution_convert_fusion.6), channel_id=1, source_target_pairs={{0,2},{1,3},{2,4},{3,5},{4,6},{5,7},{6,0},{7,1},{8,10},{9,11},{10,... | collective-permute-start | bytes 1966088 | tf_op jit(solution)/shard_map/ppermute | solution.py:211
  8.9 52.7 %collective-permute-start.6 = (bf16[256,1280]{1,0:T(8,128)(2,1)}, bf16[256,1280]{1,0:T(8,128)(2,1)S(1)}, u32[]{:S(2)}, u32[]{:S(2)}) collective-permute-start(bf16[256,1280]{1,0:T(8,128)(2,1)} %convolution_convert_fusion.2), channel_id=1, source_target_pairs={{0,6},{1,7},{2,0},{3,1},{4,2},{5,3},{6,4},{7,5},{8,14},{9,15},{10,... | collective-permute-start | bytes 1966088 | tf_op jit(solution)/shard_map/ppermute | solution.py:211
  12.8 2.8 copy-start.2
  15.7 8.9 %copy-start.7 = (s32[128,8]{0,1:T(8,128)S(1)}, s32[128,8]{0,1:T(8,128)}, u32[]{:S(2)}) copy-start(s32[128,8]{0,1:T(8,128)} %param.13) | copy-start | bytes 12292
  15.7 9.1 %copy-start.8 = (f32[128,8]{0,1:T(8,128)S(1)}, f32[128,8]{0,1:T(8,128)}, u32[]{:S(2)}) copy-start(f32[128,8]{0,1:T(8,128)} %param.14) | copy-start | bytes 12292
  15.7 22.8 %collective-permute-start.2 = (bf16[256,1280]{1,0:T(8,128)(2,1)}, bf16[256,1280]{1,0:T(8,128)(2,1)}, u32[]{:S(2)}, u32[]{:S(2)}) collective-permute-start(bf16[256,1280]{1,0:T(8,128)(2,1)} %convolution_convert_fusion.8), channel_id=1, source_target_pairs={{0,6},{1,7},{2,0},{3,1},{4,2},{5,3},{6,4},{7,5},{8,14},{9,15},{10,... | collective-permute-start | bytes 1966088 | tf_op jit(solution)/shard_map/ppermute | solution.py:211
  17.2 25.8 %collective-permute-start.4 = (bf16[256,1280]{1,0:T(8,128)(2,1)}, bf16[256,1280]{1,0:T(8,128)(2,1)}, u32[]{:S(2)}, u32[]{:S(2)}) collective-permute-start(bf16[256,1280]{1,0:T(8,128)(2,1)} %convolution_convert_fusion.9), channel_id=1, source_target_pairs={{0,2},{1,3},{2,4},{3,5},{4,6},{5,7},{6,0},{7,1},{8,10},{9,11},{10,... | collective-permute-start | bytes 1966088 | tf_op jit(solution)/shard_map/ppermute | solution.py:211
  20.8 37.0 %collective-permute-start = (bf16[512,1536]{1,0:T(8,128)(2,1)}, bf16[512,1536]{1,0:T(8,128)(2,1)}, u32[]{:S(2)}, u32[]{:S(2)}) collective-permute-start(bf16[512,1536]{1,0:T(8,128)(2,1)} %convolution_convert_fusion), channel_id=1, source_target_pairs={{0,1},{1,0},{2,3},{3,2},{4,5},{5,4},{6,7},{7,6},{8,9},{9,8},{10,11... | collective-permute-start | bytes 4718600 | tf_op jit(solution)/shard_map/ppermute | solution.py:214
  26.8 16.2 %copy-start.3 = (bf16[512,4096]{1,0:T(8,128)(2,1)S(1)}, bf16[512,4096]{1,0:T(8,128)(2,1)}, u32[]{:S(2)}) copy-start(bf16[512,4096]{1,0:T(8,128)(2,1)} %param.10) | copy-start | bytes 12582916
  40.6 25.4 %collective-permute-start.3 = (bf16[256,1280]{1,0:T(8,128)(2,1)S(1)}, bf16[256,1280]{1,0:T(8,128)(2,1)S(1)}, u32[]{:S(2)}, u32[]{:S(2)}) collective-permute-start(bf16[256,1280]{1,0:T(8,128)(2,1)S(1)} %add_convert_fusion.2), channel_id=1, source_target_pairs={{0,6},{1,7},{2,0},{3,1},{4,2},{5,3},{6,4},{7,5},{8,14},{9,15},{10,... | collective-permute-start | bytes 1966088 | tf_op jit(solution)/shard_map/ppermute | solution.py:211
  44.7 19.6 %collective-permute-start.5 = (bf16[256,1280]{1,0:T(8,128)(2,1)S(1)}, bf16[256,1280]{1,0:T(8,128)(2,1)S(1)}, u32[]{:S(2)}, u32[]{:S(2)}) collective-permute-start(bf16[256,1280]{1,0:T(8,128)(2,1)S(1)} %add_convert_fusion.1), channel_id=1, source_target_pairs={{0,2},{1,3},{2,4},{3,5},{4,6},{5,7},{6,0},{7,1},{8,10},{9,11},{10,... | collective-permute-start | bytes 1966088 | tf_op jit(solution)/shard_map/ppermute | solution.py:211
  60.3 13.5 %collective-permute-start.8 = (bf16[128,768]{1,0:T(8,128)(2,1)S(1)}, bf16[128,768]{1,0:T(8,128)(2,1)S(1)}, u32[]{:S(2)}, u32[]{:S(2)}) collective-permute-start(bf16[128,768]{1,0:T(8,128)(2,1)S(1)} %slice.52), channel_id=1, source_target_pairs={{0,2},{1,3},{2,4},{3,5},{4,6},{5,7},{6,0},{7,1},{8,10},{9,11},{10,... | collective-permute-start | bytes 589832 | tf_op jit(solution)/shard_map/ppermute | solution.py:211
  61.5 12.3 %collective-permute-start.13 = (bf16[128,768]{1,0:T(8,128)(2,1)S(1)}, bf16[128,768]{1,0:T(8,128)(2,1)S(1)}, u32[]{:S(2)}, u32[]{:S(2)}) collective-permute-start(bf16[128,768]{1,0:T(8,128)(2,1)S(1)} %slice.58), channel_id=1, source_target_pairs={{0,6},{1,7},{2,0},{3,1},{4,2},{5,3},{6,4},{7,5},{8,14},{9,15},{10,... | collective-permute-start | bytes 589832 | tf_op jit(solution)/shard_map/ppermute | solution.py:211
  64.3 6.5 %collective-permute-start.9 = (bf16[128,768]{1,0:T(8,128)(2,1)S(1)}, bf16[128,768]{1,0:T(8,128)(2,1)S(1)}, u32[]{:S(2)}, u32[]{:S(2)}) collective-permute-start(bf16[128,768]{1,0:T(8,128)(2,1)S(1)} %get-tuple-element.39), channel_id=1, source_target_pairs={{0,6},{1,7},{2,0},{3,1},{4,2},{5,3},{6,4},{7,5},{8,14},{9,15},{10,... | collective-permute-start | bytes 589832 | tf_op jit(solution)/shard_map/ppermute | solution.py:211
  65.7 7.9 %collective-permute-start.11 = (bf16[128,768]{1,0:T(8,128)(2,1)S(1)}, bf16[128,768]{1,0:T(8,128)(2,1)S(1)}, u32[]{:S(2)}, u32[]{:S(2)}) collective-permute-start(bf16[128,768]{1,0:T(8,128)(2,1)S(1)} %get-tuple-element.40), channel_id=1, source_target_pairs={{0,2},{1,3},{2,4},{3,5},{4,6},{5,7},{6,0},{7,1},{8,10},{9,11},{10,... | collective-permute-start | bytes 589832 | tf_op jit(solution)/shard_map/ppermute | solution.py:211
  66.5 7.3 %copy-start.6 = (pred[256,128]{0,1:T(8,128)(4,1)S(1)}, pred[256,128]{0,1:T(8,128)(4,1)}, u32[]{:S(2)}) copy-start(pred[256,128]{0,1:T(8,128)(4,1)} %broadcast_compare_fusion.1) | copy-start | bytes 98308
  66.6 14.2 %collective-permute-start.7 = (bf16[128,2560]{1,0:T(8,128)(2,1)S(1)}, bf16[128,2560]{1,0:T(8,128)(2,1)S(1)}, u32[]{:S(2)}, u32[]{:S(2)}) collective-permute-start(bf16[128,2560]{1,0:T(8,128)(2,1)S(1)} %fusion.19), channel_id=1, source_target_pairs={{0,1},{1,0},{2,3},{3,2},{4,5},{5,4},{6,7},{7,6},{8,9},{9,8},{10,11... | collective-permute-start | bytes 1966088 | tf_op jit(solution)/shard_map/ppermute | solution.py:214
  70.8 5.5 %collective-permute-start.10 = (bf16[128,768]{1,0:T(8,128)(2,1)S(1)}, bf16[128,768]{1,0:T(8,128)(2,1)S(1)}, u32[]{:S(2)}, u32[]{:S(2)}) collective-permute-start(bf16[128,768]{1,0:T(8,128)(2,1)S(1)} %add_convert_fusion.4), channel_id=1, source_target_pairs={{0,6},{1,7},{2,0},{3,1},{4,2},{5,3},{6,4},{7,5},{8,14},{9,15},{10,... | collective-permute-start | bytes 589832 | tf_op jit(solution)/shard_map/ppermute | solution.py:211
  73.7 6.1 %collective-permute-start.12 = (bf16[128,768]{1,0:T(8,128)(2,1)S(1)}, bf16[128,768]{1,0:T(8,128)(2,1)S(1)}, u32[]{:S(2)}, u32[]{:S(2)}) collective-permute-start(bf16[128,768]{1,0:T(8,128)(2,1)S(1)} %add_convert_fusion.3), channel_id=1, source_target_pairs={{0,2},{1,3},{2,4},{3,5},{4,6},{5,7},{6,0},{7,1},{8,10},{9,11},{10,... | collective-permute-start | bytes 589832 | tf_op jit(solution)/shard_map/ppermute | solution.py:211
  80.0 1.2 copy-start
  80.1 1.2 copy-start.1
  81.3 139.8 %slice-start = ((s8[6291456]{0:T(1024)(128)(4,1)}), s8[4194304]{0:T(1024)(128)(4,1)S(1)}, s32[]{:S(2)}) async-start(s8[6291456]{0:T(1024)(128)(4,1)} %bitcast.53), calls=%async_computation.2 | async-start | bytes 8388608
  81.3 139.8 %slice-start.2 = ((s8[6291456]{0:T(1024)(128)(4,1)}), s8[2097152]{0:T(1024)(128)(4,1)S(1)}, s32[]{:S(2)}) async-start(s8[6291456]{0:T(1024)(128)(4,1)} %bitcast.56), calls=%async_computation.4 | async-start | bytes 4194304
  81.3 139.8 %slice-start.4 = ((s8[6291456]{0:T(1024)(128)(4,1)}), s8[2097152]{0:T(1024)(128)(4,1)S(1)}, s32[]{:S(2)}) async-start(s8[6291456]{0:T(1024)(128)(4,1)} %bitcast.59), calls=%async_computation.6 | async-start | bytes 4194304
  89.0 132.1 %slice-start.1 = ((s8[6291456]{0:T(1024)(128)(4,1)}), s8[2097152]{0:T(1024)(128)(4,1)S(1)}, s32[]{:S(2)}) async-start(s8[6291456]{0:T(1024)(128)(4,1)} %bitcast.53), calls=%async_computation.3 | async-start | bytes 4194304
  89.0 132.1 %slice-start.3 = ((s8[6291456]{0:T(1024)(128)(4,1)}), s8[4194304]{0:T(1024)(128)(4,1)S(1)}, s32[]{:S(2)}) async-start(s8[6291456]{0:T(1024)(128)(4,1)} %bitcast.56), calls=%async_computation.5 | async-start | bytes 8388608
  89.0 132.1 %slice-start.5 = ((s8[6291456]{0:T(1024)(128)(4,1)}), s8[4194304]{0:T(1024)(128)(4,1)S(1)}, s32[]{:S(2)}) async-start(s8[6291456]{0:T(1024)(128)(4,1)} %bitcast.59), calls=%async_computation.7 | async-start | bytes 8388608

commit v4 on v3

--- a/solution.py
+++ b/solution.py
@@ -95,7 +95,7 @@
             jax.ShapeDtypeStruct((toks, width), F32),
         ],
         scratch_shapes=[pltpu.VMEM((PIECES, toks, tile), BF16)],
-        compiler_params=pltpu.CompilerParams(vmem_limit_bytes=VMEM),
+        compiler_params=pltpu.CompilerParams(vmem_limit_bytes=26 * 2**20),
         cost_estimate=pl.CostEstimate(flops=3 * 10**9, bytes_accessed=15 * 10**6, transcendentals=0),
         name="build_rows",
     )(slot, near, far, residual, gain)
@@ -229,31 +229,29 @@
     up_two, down_two = times(far_rows[2], mid, first), times(far_rows[2], 0, mid)
     z_rows = pick(by_z, 1 - z).reshape(4 * toks, -1)
     up_two, down_two, z_rows = lax.optimization_barrier((up_two, down_two, z_rows))
+    z_chunk = times(z_rows, first, width)
+    z_chunk, up_rows, down_rows = lax.optimization_barrier((z_chunk, far_rows[1], far_rows[3]))
+    up_one, down_one = times(up_rows, 0, mid), times(down_rows, mid, first)
+    up_one, down_one, up_rows, down_rows = lax.optimization_barrier((up_one, down_one, up_rows, down_rows))
     up_far, down_far = along_x(up_two, 1), along_x(down_two, -1)
-    away = along_z(times(z_rows, first, width))
-    up_near = along_x(times(far_rows[1], 0, mid), 1)
-    down_near = along_x(times(far_rows[3], mid, first), -1)
-    up_sum = along_x(add(dot(far_rows[1], out_weight[:, mid:first]).astype(BF16), up_far), 1)
-    down_sum = along_x(add(dot(far_rows[3], out_weight[:, :mid]).astype(BF16), down_far), -1)
+    away = along_z(z_chunk)
+    up_near, down_near = along_x(up_one, 1), along_x(down_one, -1)
+    up_sum = along_x(add(times(up_rows, mid, first), up_far), 1)
+    down_sum = along_x(add(times(down_rows, 0, mid), down_far), -1)
 
     own = times(pick(by_z, z).reshape(4 * toks, -1), first, width)
     both = add(own, away)
     both, own_rows = lax.optimization_barrier((both, far_rows[0]))
     both = both.reshape(4, toks, width - first)
     chunk = [pick(both, (x + d) % 4) for d in range(4)]
-    half = (width - first) // 2
-    b_up_far, b_down_far = along_x(chunk[2][:, half:], 1), along_x(chunk[2][:, :half], -1)
-    b_up_near, b_down_near = along_x(chunk[1][:, :half], 1), along_x(chunk[3][:, half:], -1)
-    b_up_sum = along_x(add(chunk[1][:, half:], b_up_far), 1)
-    b_down_sum = along_x(add(chunk[3][:, :half], b_down_far), -1)
+    from_down, from_up, from_two = along_x(chunk[1], 1), along_x(chunk[3], -1), along_x(chunk[2], 2)
 
     left = times(own_rows, 0, mid).astype(F32) + up_near.astype(F32) + down_sum.astype(F32)
     right = times(own_rows, mid, first).astype(F32) + up_sum.astype(F32) + down_near.astype(F32)
     near = jnp.concatenate([left, right], axis=1).reshape(2, toks, first)
     near = pick(near, z) + along_z(pick(near, 1 - z).astype(BF16)).astype(F32)
-    b_left = chunk[0][:, :half].astype(F32) + b_up_near.astype(F32) + b_down_sum.astype(F32)
-    b_right = chunk[0][:, half:].astype(F32) + b_up_sum.astype(F32) + b_down_near.astype(F32)
-    return near, jnp.concatenate([b_left, b_right], axis=1)
+    far = chunk[0].astype(F32) + from_down.astype(F32) + from_up.astype(F32) + from_two.astype(F32)
+    return near, far
 
 
 def shards(attn_heads, out_weight, residual, norm_gain, expert_ids, gate_probs, expert_gate, expert_up, expert_down):

time: 383 us -> 379 us (0.990)
  waiting for transfers between devices: 32.8 us -> 38.4 us
    ppermute x2, waiting for transfers between devices: 13.8 us -> 25.2 us  [along_z(): return lax.ppermute(v, 'tensor', [(i, i ^ 1) for i in range(8)])]
    ppermute x12 -> x9, waiting for transfers between devices: 19 us -> 13.2 us  [along_x(): lax.ppermute(v, 'tensor', [(i * 2 + j, (i + by) % 4 * 2 + j) for i in ran...]
    ppermute x12 -> x9, starting transfers between devices: 14.6 us -> 11.6 us  [along_x(): lax.ppermute(v, 'tensor', [(i * 2 + j, (i + by) % 4 * 2 + j) for i in ran...]
  transfers between devices with their start and end apart: 14 -> 11, of which waited for: 6 -> 4; matrix products, arithmetic and copies ran while one was open for 6% -> 4% of each run, Pallas kernels for 0% -> 0%
where the time goes in v4:
time: 379 us
  blocking collectives  255 us (67%)
  Pallas kernels  41 us (11%)
  waiting for transfers between devices  38.4 us (10%)
  matrix products  19.2 us (5%)
  starting transfers between devices  18.2 us (5%)
  local copies, waits for them, and re-layouts  4.96 us (1%)
    all_to_all x2, blocking collectives, swap(): lax.all_to_all(v.reshape(experts, MAIN, cols), ('dp', 'tensor'), split_ax...  255 us
    pallas_call x1, Pallas kernels, expert(): pl.pallas_call(kernel, grid=(flat // block,), in_specs=[pl.BlockSpec((blo...  28.8 us
    ppermute x2, waiting for transfers between devices, along_z(): return lax.ppermute(v, 'tensor', [(i, i ^ 1) for i in range(8)])  25.2 us
    dot_general x11, matrix products, dot(): return jnp.dot(a, b, preferred_element_type=F32)  19.2 us
    ppermute x9, waiting for transfers between devices, along_x(): lax.ppermute(v, 'tensor', [(i * 2 + j, (i + by) % 4 * 2 + j) for i in ran...  13.2 us
    ppermute x9, starting transfers between devices, along_x(): lax.ppermute(v, 'tensor', [(i * 2 + j, (i + by) % 4 * 2 + j) for i in ran...  11.6 us
  transfers between devices with their start and end apart: 11, of which 4 were waited for; matrix products, arithmetic and copies ran while one was open for 4% of the time, Pallas kernels for 0%

profile of v4, /device:TPU:1, one launch (start us, length us, event | category | flops | bytes accessed | tf_op | source)
XLA Modules:
  0.0 379.1 jit_solution(7109170004313218770)
XLA Ops:
  0.0 1.3 constant_dynamic-slice_fusion
  1.3 2.8 convolution_convert_fusion.8
  4.1 2.7 convolution_convert_fusion.9
  6.8 0.9 constant_dynamic-slice_fusion.5
  7.7 3.3 collective-permute-start.2
  11.0 3.6 convolution_convert_fusion
  14.6 1.4 convolution_convert_fusion.6
  16.0 1.4 convolution_convert_fusion.5
  17.4 0.2 collective-permute-start.1
  17.6 2.5 collective-permute-start.6
  20.0 3.6 collective-permute-start
  23.7 0.1 fusion.6.slot_ref
  24.0 0.1 eq.75
  24.2 0.1 eq.69
  24.3 0.1 copy.18
  24.4 0.2 copy.16
  24.6 0.1 broadcast_compare_fusion
  25.0 0.1 copy.19
  25.1 0.2 copy.17
  25.4 0.4 copy-done.7
  25.7 2.2 add_convert_fusion.2
  28.0 2.3 collective-permute-start.3
  30.3 1.6 add_convert_fusion.1
  31.9 0.1 collective-permute-start.5
  31.9 25.2 %collective-permute-done = bf16[512,1536]{1,0:T(8,128)(2,1)} collective-permute-done((bf16[512,1536]{1,0:T(8,128)(2,1)}, bf16[512,1536]{1,0:T(8,128)(2,1)}, u32[]{:S(2)}, u32[]{:S(2)}) %collective-permute-start) | collective-permute-done | bytes 1572896 | tf_op jit(solution)/shard_map/ppermute | solution.py:214
  57.1 2.4 add_convert_fusion
  59.6 0.5 fusion.2
  60.1 0.5 fusion
  60.6 0.1 dynamic-slice_bitcast_fusion.2
  60.7 0.1 collective-permute-start.8
  60.8 2.3 collective-permute-start.10
  63.2 0.9 collective-permute-start.9
  64.1 0.2 convert_add_fusion
  64.3 0.2 convert_add_fusion.1
  64.5 0.3 pad_maximum_fusion
  64.8 0.1 fusion.21
  64.9 2.9 collective-permute-start.7
  67.9 3.2 collective-permute-done.8
  71.0 7.3 %collective-permute-done.10 = bf16[128,1536]{1,0:T(8,128)(2,1)S(1)} collective-permute-done((bf16[128,1536]{1,0:T(8,128)(2,1)S(1)}, bf16[128,1536]{1,0:T(8,128)(2,1)S(1)}, u32[]{:S(2)}, u32[]{:S(2)}) %collective-permute-start.10) | collective-permute-done | bytes 393248 | tf_op jit(solution)/shard_map/ppermute | solution.py:211
  78.3 2.7 collective-permute-done.9
  81.0 0.2 fusion.20.far_ref
  81.3 0.1 bitcast_add_fusion.near_ref
  81.4 1.0 copy-done
  82.5 5.7 %build_rows.1 = (bf16[1024,5120]{1,0:T(8,128)(2,1)S(1)}, f32[128,4096]{1,0:T(8,128)S(1)}) custom-call(s32[128,128]{1,0:T(8,128)S(1)} %fusion.6.slot_ref, f32[128,2560]{1,0:T(8,128)S(1)} %bitcast_add_fusion.near_ref, f32[128,1536]{1,0:T(8,128)S(1)} %fusion.20.far_ref, bf16[128,4096]{1,0:T(8,128)(2,1)S(1)} %copy-done, f32[1,4096]{1,0:T(1,128)S(1)} %bitcast.64), custom_call_target="tpu_custom_call" | custom-call | flops 3000000000 | bytes 15000000 | tf_op jit(solution)/shard_map/build_rows/pallas_call | solution.py:82
  88.3 128.9 %all_to_all.10 = bf16[128,8,5120]{2,1,0:T(8,128)(2,1)} all-to-all(bf16[128,8,5120]{2,1,0:T(8,128)(2,1)S(1)} %bitcast.54), channel_id=1, replica_groups=mesh['dp'=16,'tensor'=8] {'dp','tensor'}, dimensions={0} | all-to-all | bytes 20971520 | tf_op jit(solution)/shard_map/all_to_all | solution.py:269
  217.3 28.8 %expert_rows.1 = bf16[1024,5120]{1,0:T(8,128)(2,1)} custom-call(bf16[1024,5120]{1,0:T(8,128)(2,1)} %bitcast.65, bf16[4096,768]{1,0:T(8,128)(2,1)S(1)} %bitcast.57, bf16[4096,768]{1,0:T(8,128)(2,1)S(1)} %bitcast.60, bf16[768,4096]{1,0:T(8,128)(2,1)S(1)} %bitcast.63), custom_call_target="tpu_custom_call" | custom-call | flops 24000000000 | bytes 40000000 | tf_op jit(solution)/shard_map/expert_rows/pallas_call | solution.py:135
  246.1 126.5 %all_to_all.11 = bf16[128,8,5120]{2,1,0:T(8,128)(2,1)S(1)} all-to-all(bf16[128,8,5120]{2,1,0:T(8,128)(2,1)} %bitcast.66), channel_id=1, replica_groups=mesh['dp'=16,'tensor'=8] {'dp','tensor'}, dimensions={0} | all-to-all | bytes 20971520 | tf_op jit(solution)/shard_map/all_to_all | solution.py:269
  372.6 6.5 %combine_rows.1 = bf16[128,4096]{1,0:T(8,128)(2,1)} custom-call(bf16[256,1024]{1,0:T(8,128)(2,1)S(1)} %fusion.22.main_w_ref, bf16[256,256]{1,0:T(8,128)(2,1)S(1)} %fusion.24.spill_w_ref, bf16[1024,5120]{1,0:T(8,128)(2,1)S(1)} %bitcast.52, bf16[1024,5120]{1,0:T(8,128)(2,1)S(1)} %bitcast.53, f32[128,4096]{1,0:T(8,128)S(1)} %get-tuple-element.38.hidden_ref), custom_call_target="tpu_custom_call" | custom-call | flops 4000000000 | bytes 15000000 | tf_op jit(solution)/shard_map/combine_rows/pallas_call | solution.py:181
  (56 shorter events, 0.6 us)
Async XLA Ops:
  1.3 14.7 %copy-start.6 = (bf16[1,2,128,512]{3,2,1,0:T(8,128)(2,1)}, bf16[1,2,128,512]{3,2,1,0:T(8,128)(2,1)S(1)}, u32[]{:S(2)}) copy-start(bf16[1,2,128,512]{3,2,1,0:T(8,128)(2,1)S(1)} %get-tuple-element.45) | copy-start | bytes 786436
  4.1 2.7 copy-start.2
  7.7 6.9 %copy-start.3 = (bf16[512,4096]{1,0:T(8,128)(2,1)S(1)}, bf16[512,4096]{1,0:T(8,128)(2,1)}, u32[]{:S(2)}) copy-start(bf16[512,4096]{1,0:T(8,128)(2,1)} %param.10) | copy-start | bytes 12582916
  7.7 17.6 %collective-permute-start.2 = (bf16[256,1280]{1,0:T(8,128)(2,1)}, bf16[256,1280]{1,0:T(8,128)(2,1)}, u32[]{:S(2)}, u32[]{:S(2)}) collective-permute-start(bf16[256,1280]{1,0:T(8,128)(2,1)} %convolution_convert_fusion.8), channel_id=1, source_target_pairs={{0,6},{1,7},{2,0},{3,1},{4,2},{5,3},{6,4},{7,5},{8,14},{9,15},{10,... | collective-permute-start | bytes 1966088 | tf_op jit(solution)/shard_map/ppermute | solution.py:211
  11.0 19.2 %collective-permute-start.4 = (bf16[256,1280]{1,0:T(8,128)(2,1)}, bf16[256,1280]{1,0:T(8,128)(2,1)}, u32[]{:S(2)}, u32[]{:S(2)}) collective-permute-start(bf16[256,1280]{1,0:T(8,128)(2,1)} %convolution_convert_fusion.9), channel_id=1, source_target_pairs={{0,2},{1,3},{2,4},{3,5},{4,6},{5,7},{6,0},{7,1},{8,10},{9,11},{10,... | collective-permute-start | bytes 1966088 | tf_op jit(solution)/shard_map/ppermute | solution.py:211
  16.0 7.6 %copy-start.8 = (s32[128,8]{0,1:T(8,128)S(1)}, s32[128,8]{0,1:T(8,128)}, u32[]{:S(2)}) copy-start(s32[128,8]{0,1:T(8,128)} %param.13) | copy-start | bytes 12292
  16.0 7.9 %copy-start.9 = (f32[128,8]{0,1:T(8,128)S(1)}, f32[128,8]{0,1:T(8,128)}, u32[]{:S(2)}) copy-start(f32[128,8]{0,1:T(8,128)} %param.14) | copy-start | bytes 12292
  17.4 46.9 %collective-permute-start.1 = (bf16[256,1280]{1,0:T(8,128)(2,1)}, bf16[256,1280]{1,0:T(8,128)(2,1)S(1)}, u32[]{:S(2)}, u32[]{:S(2)}) collective-permute-start(bf16[256,1280]{1,0:T(8,128)(2,1)} %convolution_convert_fusion.6), channel_id=1, source_target_pairs={{0,2},{1,3},{2,4},{3,5},{4,6},{5,7},{6,0},{7,1},{8,10},{9,11},{10,... | collective-permute-start | bytes 1966088 | tf_op jit(solution)/shard_map/ppermute | solution.py:211
  17.6 43.3 %collective-permute-start.6 = (bf16[256,1280]{1,0:T(8,128)(2,1)}, bf16[256,1280]{1,0:T(8,128)(2,1)S(1)}, u32[]{:S(2)}, u32[]{:S(2)}) collective-permute-start(bf16[256,1280]{1,0:T(8,128)(2,1)} %convolution_convert_fusion.5), channel_id=1, source_target_pairs={{0,6},{1,7},{2,0},{3,1},{4,2},{5,3},{6,4},{7,5},{8,14},{9,15},{10,... | collective-permute-start | bytes 1966088 | tf_op jit(solution)/shard_map/ppermute | solution.py:211
  20.0 37.1 %collective-permute-start = (bf16[512,1536]{1,0:T(8,128)(2,1)}, bf16[512,1536]{1,0:T(8,128)(2,1)}, u32[]{:S(2)}, u32[]{:S(2)}) collective-permute-start(bf16[512,1536]{1,0:T(8,128)(2,1)} %convolution_convert_fusion), channel_id=1, source_target_pairs={{0,1},{1,0},{2,3},{3,2},{4,5},{5,4},{6,7},{7,6},{8,9},{9,8},{10,11... | collective-permute-start | bytes 4718600 | tf_op jit(solution)/shard_map/ppermute | solution.py:214
  24.8 1.0 copy-start.7
  25.3 5.0 %copy-start.4 = (bf16[512,4096]{1,0:T(8,128)(2,1)S(1)}, bf16[512,4096]{1,0:T(8,128)(2,1)}, u32[]{:S(2)}) copy-start(bf16[512,4096]{1,0:T(8,128)(2,1)} %param.10) | copy-start | bytes 12582916
  28.0 29.2 %copy-start.5 = (bf16[4,1,128,512]{3,2,1,0:T(8,128)(2,1)S(1)}, bf16[4,1,128,512]{3,2,1,0:T(8,128)(2,1)}, u32[]{:S(2)}) copy-start(bf16[4,1,128,512]{3,2,1,0:T(8,128)(2,1)} %get-tuple-element.48) | copy-start | bytes 1572868
  28.0 36.3 %collective-permute-start.3 = (bf16[256,1280]{1,0:T(8,128)(2,1)S(1)}, bf16[256,1280]{1,0:T(8,128)(2,1)S(1)}, u32[]{:S(2)}, u32[]{:S(2)}) collective-permute-start(bf16[256,1280]{1,0:T(8,128)(2,1)S(1)} %add_convert_fusion.2), channel_id=1, source_target_pairs={{0,6},{1,7},{2,0},{3,1},{4,2},{5,3},{6,4},{7,5},{8,14},{9,15},{10,... | collective-permute-start | bytes 1966088 | tf_op jit(solution)/shard_map/ppermute | solution.py:211
  31.9 31.3 %collective-permute-start.5 = (bf16[256,1280]{1,0:T(8,128)(2,1)S(1)}, bf16[256,1280]{1,0:T(8,128)(2,1)S(1)}, u32[]{:S(2)}, u32[]{:S(2)}) collective-permute-start(bf16[256,1280]{1,0:T(8,128)(2,1)S(1)} %add_convert_fusion.1), channel_id=1, source_target_pairs={{0,2},{1,3},{2,4},{3,5},{4,6},{5,7},{6,0},{7,1},{8,10},{9,11},{10,... | collective-permute-start | bytes 1966088 | tf_op jit(solution)/shard_map/ppermute | solution.py:211
  60.7 10.3 %collective-permute-start.8 = (bf16[128,1536]{1,0:T(8,128)(2,1)S(1)}, bf16[128,1536]{1,0:T(8,128)(2,1)S(1)}, u32[]{:S(2)}, u32[]{:S(2)}) collective-permute-start(bf16[128,1536]{1,0:T(8,128)(2,1)S(1)} %get-tuple-element.41), channel_id=1, source_target_pairs={{0,2},{1,3},{2,4},{3,5},{4,6},{5,7},{6,0},{7,1},{8,10},{9,11},{10,... | collective-permute-start | bytes 1179656 | tf_op jit(solution)/shard_map/ppermute | solution.py:211
  60.8 17.5 %collective-permute-start.10 = (bf16[128,1536]{1,0:T(8,128)(2,1)S(1)}, bf16[128,1536]{1,0:T(8,128)(2,1)S(1)}, u32[]{:S(2)}, u32[]{:S(2)}) collective-permute-start(bf16[128,1536]{1,0:T(8,128)(2,1)S(1)} %get-tuple-element.42), channel_id=1, source_target_pairs={{0,4},{1,5},{2,6},{3,7},{4,0},{5,1},{6,2},{7,3},{8,12},{9,13},{10,... | collective-permute-start | bytes 1179656 | tf_op jit(solution)/shard_map/ppermute | solution.py:211
  63.2 17.9 %collective-permute-start.9 = (bf16[128,1536]{1,0:T(8,128)(2,1)S(1)}, bf16[128,1536]{1,0:T(8,128)(2,1)S(1)}, u32[]{:S(2)}, u32[]{:S(2)}) collective-permute-start(bf16[128,1536]{1,0:T(8,128)(2,1)S(1)} %get-tuple-element.43), channel_id=1, source_target_pairs={{0,6},{1,7},{2,0},{3,1},{4,2},{5,3},{6,4},{7,5},{8,14},{9,15},{10,... | collective-permute-start | bytes 1179656 | tf_op jit(solution)/shard_map/ppermute | solution.py:211
  64.9 16.4 %collective-permute-start.7 = (bf16[128,2560]{1,0:T(8,128)(2,1)S(1)}, bf16[128,2560]{1,0:T(8,128)(2,1)S(1)}, u32[]{:S(2)}, u32[]{:S(2)}) collective-permute-start(bf16[128,2560]{1,0:T(8,128)(2,1)S(1)} %fusion.21), channel_id=1, source_target_pairs={{0,1},{1,0},{2,3},{3,2},{4,5},{5,4},{6,7},{7,6},{8,9},{9,8},{10,11... | collective-permute-start | bytes 1966088 | tf_op jit(solution)/shard_map/ppermute | solution.py:214
  81.2 1.2 copy-start
  81.2 1.2 copy-start.1
  82.5 134.7 %slice-start = ((s8[6291456]{0:T(1024)(128)(4,1)}), s8[4194304]{0:T(1024)(128)(4,1)S(1)}, s32[]{:S(2)}) async-start(s8[6291456]{0:T(1024)(128)(4,1)} %bitcast.55), calls=%async_computation.2 | async-start | bytes 8388608
  82.5 134.7 %slice-start.2 = ((s8[6291456]{0:T(1024)(128)(4,1)}), s8[2097152]{0:T(1024)(128)(4,1)S(1)}, s32[]{:S(2)}) async-start(s8[6291456]{0:T(1024)(128)(4,1)} %bitcast.58), calls=%async_computation.4 | async-start | bytes 4194304
  82.5 134.7 %slice-start.4 = ((s8[6291456]{0:T(1024)(128)(4,1)}), s8[4194304]{0:T(1024)(128)(4,1)S(1)}, s32[]{:S(2)}) async-start(s8[6291456]{0:T(1024)(128)(4,1)} %bitcast.61), calls=%async_computation.6 | async-start | bytes 8388608
  88.2 129.0 %slice-start.1 = ((s8[6291456]{0:T(1024)(128)(4,1)}), s8[2097152]{0:T(1024)(128)(4,1)S(1)}, s32[]{:S(2)}) async-start(s8[6291456]{0:T(1024)(128)(4,1)} %bitcast.55), calls=%async_computation.3 | async-start | bytes 4194304
  88.2 129.0 %slice-start.3 = ((s8[6291456]{0:T(1024)(128)(4,1)}), s8[4194304]{0:T(1024)(128)(4,1)S(1)}, s32[]{:S(2)}) async-start(s8[6291456]{0:T(1024)(128)(4,1)} %bitcast.58), calls=%async_computation.5 | async-start | bytes 8388608
  88.2 129.0 %slice-start.5 = ((s8[6291456]{0:T(1024)(128)(4,1)}), s8[2097152]{0:T(1024)(128)(4,1)S(1)}, s32[]{:S(2)}) async-start(s8[6291456]{0:T(1024)(128)(4,1)} %bitcast.61), calls=%async_computation.7 | async-start | bytes 4194304

commit v5 on v4

--- a/solution.py
+++ b/solution.py
@@ -230,14 +230,13 @@
     z_rows = pick(by_z, 1 - z).reshape(4 * toks, -1)
     up_two, down_two, z_rows = lax.optimization_barrier((up_two, down_two, z_rows))
     z_chunk = times(z_rows, first, width)
-    z_chunk, up_rows, down_rows = lax.optimization_barrier((z_chunk, far_rows[1], far_rows[3]))
-    up_one, down_one = times(up_rows, 0, mid), times(down_rows, mid, first)
-    up_one, down_one, up_rows, down_rows = lax.optimization_barrier((up_one, down_one, up_rows, down_rows))
     up_far, down_far = along_x(up_two, 1), along_x(down_two, -1)
     away = along_z(z_chunk)
-    up_near, down_near = along_x(up_one, 1), along_x(down_one, -1)
-    up_sum = along_x(add(times(up_rows, mid, first), up_far), 1)
-    down_sum = along_x(add(times(down_rows, 0, mid), down_far), -1)
+    z_chunk, up_rows, down_rows = lax.optimization_barrier((z_chunk, far_rows[1], far_rows[3]))
+    up_one, down_one = dot(up_rows, out_weight[:, :first]), dot(down_rows, out_weight[:, :first])
+    up_one, down_one, up_far, down_far = lax.optimization_barrier((up_one, down_one, up_far, down_far))
+    up_got = along_x(jnp.concatenate([up_one[:, :mid], up_one[:, mid:] + up_far.astype(F32)], axis=1).astype(BF16), 1)
+    down_got = along_x(jnp.concatenate([down_one[:, :mid] + down_far.astype(F32), down_one[:, mid:]], axis=1).astype(BF16), -1)
 
     own = times(pick(by_z, z).reshape(4 * toks, -1), first, width)
     both = add(own, away)
@@ -246,9 +245,8 @@
     chunk = [pick(both, (x + d) % 4) for d in range(4)]
     from_down, from_up, from_two = along_x(chunk[1], 1), along_x(chunk[3], -1), along_x(chunk[2], 2)
 
-    left = times(own_rows, 0, mid).astype(F32) + up_near.astype(F32) + down_sum.astype(F32)
-    right = times(own_rows, mid, first).astype(F32) + up_sum.astype(F32) + down_near.astype(F32)
-    near = jnp.concatenate([left, right], axis=1).reshape(2, toks, first)
+    near = times(own_rows, 0, first).astype(F32) + up_got.astype(F32) + down_got.astype(F32)
+    near = near.reshape(2, toks, first)
     near = pick(near, z) + along_z(pick(near, 1 - z).astype(BF16)).astype(F32)
     far = chunk[0].astype(F32) + from_down.astype(F32) + from_up.astype(F32) + from_two.astype(F32)
     return near, far

time: 379 us -> 377 us (level)
  blocking collectives: 255 us -> 260 us
    all_to_all x2, blocking collectives: 255 us -> 260 us  [swap(): lax.all_to_all(v.reshape(experts, MAIN, cols), ('dp', 'tensor'), split_ax...]
    dot_general x11 -> x8, matrix products: 19.2 us -> 16 us  [dot(): return jnp.dot(a, b, preferred_element_type=F32)]
    ppermute x9 -> x7, starting transfers between devices: 11.6 us -> 9.48 us  [along_x(): lax.ppermute(v, 'tensor', [(i * 2 + j, (i + by) % 4 * 2 + j) for i in ran...]
    ppermute x9 -> x7, waiting for transfers between devices: 13.2 us -> 13.3 us  [along_x(): lax.ppermute(v, 'tensor', [(i * 2 + j, (i + by) % 4 * 2 + j) for i in ran...]
  transfers between devices with their start and end apart: 11 -> 9, of which waited for: 4 -> 5; matrix products, arithmetic and copies ran while one was open for 4% -> 4% of each run, Pallas kernels for 0% -> 0%
where the time goes in v5:
time: 377 us
  blocking collectives  260 us (69%)
  Pallas kernels  41 us (11%)
  waiting for transfers between devices  35.6 us (9%)
  starting transfers between devices  17.6 us (5%)
  matrix products  16 us (4%)
  local copies, waits for them, and re-layouts  3.89 us (1%)
    all_to_all x2, blocking collectives, swap(): lax.all_to_all(v.reshape(experts, MAIN, cols), ('dp', 'tensor'), split_ax...  260 us
    pallas_call x1, Pallas kernels, expert(): pl.pallas_call(kernel, grid=(flat // block,), in_specs=[pl.BlockSpec((blo...  28.8 us
    ppermute x2, waiting for transfers between devices, along_z(): return lax.ppermute(v, 'tensor', [(i, i ^ 1) for i in range(8)])  22.3 us
    dot_general x8, matrix products, dot(): return jnp.dot(a, b, preferred_element_type=F32)  16 us
    ppermute x7, waiting for transfers between devices, along_x(): lax.ppermute(v, 'tensor', [(i * 2 + j, (i + by) % 4 * 2 + j) for i in ran...  13.3 us
    ppermute x7, starting transfers between devices, along_x(): lax.ppermute(v, 'tensor', [(i * 2 + j, (i + by) % 4 * 2 + j) for i in ran...  9.48 us
    ppermute x2, starting transfers between devices, along_z(): return lax.ppermute(v, 'tensor', [(i, i ^ 1) for i in range(8)])  8.08 us
  transfers between devices with their start and end apart: 9, of which 5 were waited for; matrix products, arithmetic and copies ran while one was open for 4% of the time, Pallas kernels for 0%

profile of v5, /device:TPU:1, one launch (start us, length us, event | category | flops | bytes accessed | tf_op | source)
XLA Modules:
  0.0 376.9 jit_solution(16013186150771183447)
XLA Ops:
  0.0 1.3 constant_dynamic-slice_fusion.2
  1.3 2.7 convolution_convert_fusion.3
  4.1 2.7 convolution_convert_fusion.4
  6.7 0.9 constant_dynamic-slice_fusion.5
  7.6 2.0 collective-permute-start.1
  9.6 1.3 collective-permute-start.2
  10.9 3.5 convolution_convert_fusion.1
  14.5 3.8 %collective-permute-start = (bf16[512,1536]{1,0:T(8,128)(2,1)}, bf16[512,1536]{1,0:T(8,128)(2,1)}, u32[]{:S(2)}, u32[]{:S(2)}) collective-permute-start(bf16[512,1536]{1,0:T(8,128)(2,1)} %convolution_convert_fusion.1), channel_id=1, source_target_pairs={{0,1},{1,0},{2,3},{3,2},{4,5},{5,4},{6,7},{7,6},{8,9},{9,8},{10,11... | collective-permute-start | bytes 4718600 | tf_op jit(solution)/shard_map/ppermute | solution.py:214
  18.3 0.1 fusion.12.slot_ref
  18.5 0.1 eq.75
  18.7 0.1 eq.69
  18.9 0.1 broadcast_in_dim.64
  19.1 0.1 copy.19
  19.3 0.1 copy.18
  19.4 0.2 copy.17
  19.6 0.2 copy.16
  19.8 2.7 fusion.3
  22.5 0.2 copy-done.2
  22.8 0.8 fusion.1
  23.6 1.6 collective-permute-done.1
  25.2 0.1 slice.60
  25.3 0.1 slice.59
  25.4 1.3 add_convert_fusion.1
  26.7 0.1 pad_maximum_fusion.1
  26.8 2.4 collective-permute-start.4
  29.2 0.2 add_convert_fusion.2
  29.4 0.1 pad_maximum_fusion
  29.5 0.1 collective-permute-start.3
  29.6 0.1 broadcast_compare_fusion
  29.7 22.3 %collective-permute-done = bf16[512,1536]{1,0:T(8,128)(2,1)} collective-permute-done((bf16[512,1536]{1,0:T(8,128)(2,1)}, bf16[512,1536]{1,0:T(8,128)(2,1)}, u32[]{:S(2)}, u32[]{:S(2)}) %collective-permute-start) | collective-permute-done | bytes 1572896 | tf_op jit(solution)/shard_map/ppermute | solution.py:214
  52.0 2.4 add_convert_fusion
  54.5 0.1 dynamic-slice_bitcast_fusion.2
  54.6 0.1 collective-permute-start.6
  54.7 2.4 collective-permute-start.8
  57.1 1.2 collective-permute-start.7
  58.3 0.5 collective-permute-done.3
  58.8 0.9 convert_add_fusion
  59.7 0.1 fusion.15
  59.7 4.3 %collective-permute-start.5 = (bf16[128,2560]{1,0:T(8,128)(2,1)S(1)}, bf16[128,2560]{1,0:T(8,128)(2,1)S(1)}, u32[]{:S(2)}, u32[]{:S(2)}) collective-permute-start(bf16[128,2560]{1,0:T(8,128)(2,1)S(1)} %fusion.15), channel_id=1, source_target_pairs={{0,1},{1,0},{2,3},{3,2},{4,5},{5,4},{6,7},{7,6},{8,9},{9,8},{10,11... | collective-permute-start | bytes 1966088 | tf_op jit(solution)/shard_map/ppermute | solution.py:214
  64.1 3.4 collective-permute-done.6
  67.5 7.8 %collective-permute-done.8 = bf16[128,1536]{1,0:T(8,128)(2,1)S(1)} collective-permute-done((bf16[128,1536]{1,0:T(8,128)(2,1)S(1)}, bf16[128,1536]{1,0:T(8,128)(2,1)S(1)}, u32[]{:S(2)}, u32[]{:S(2)}) %collective-permute-start.8) | collective-permute-done | bytes 393248 | tf_op jit(solution)/shard_map/ppermute | solution.py:211
  75.3 0.2 fusion.14.far_ref
  75.6 0.1 bitcast_add_fusion.near_ref
  75.8 5.7 %build_rows.1 = (bf16[1024,5120]{1,0:T(8,128)(2,1)S(1)}, f32[128,4096]{1,0:T(8,128)S(1)}) custom-call(s32[128,128]{1,0:T(8,128)S(1)} %fusion.12.slot_ref, f32[128,2560]{1,0:T(8,128)S(1)} %bitcast_add_fusion.near_ref, f32[128,1536]{1,0:T(8,128)S(1)} %fusion.14.far_ref, bf16[128,4096]{1,0:T(8,128)(2,1)S(1)} %copy-done, f32[1,4096]{1,0:T(1,128)S(1)} %bitcast.61), custom_call_target="tpu_custom_call" | custom-call | flops 3000000000 | bytes 15000000 | tf_op jit(solution)/shard_map/build_rows/pallas_call | solution.py:82
  81.6 133.5 %all_to_all.10 = bf16[128,8,5120]{2,1,0:T(8,128)(2,1)} all-to-all(bf16[128,8,5120]{2,1,0:T(8,128)(2,1)S(1)} %bitcast.51), channel_id=1, replica_groups=mesh['dp'=16,'tensor'=8] {'dp','tensor'}, dimensions={0} | all-to-all | bytes 20971520 | tf_op jit(solution)/shard_map/all_to_all | solution.py:267
  215.1 28.8 %expert_rows.1 = bf16[1024,5120]{1,0:T(8,128)(2,1)} custom-call(bf16[1024,5120]{1,0:T(8,128)(2,1)} %bitcast.62, bf16[4096,768]{1,0:T(8,128)(2,1)S(1)} %bitcast.54, bf16[4096,768]{1,0:T(8,128)(2,1)S(1)} %bitcast.57, bf16[768,4096]{1,0:T(8,128)(2,1)S(1)} %bitcast.60), custom_call_target="tpu_custom_call" | custom-call | flops 24000000000 | bytes 40000000 | tf_op jit(solution)/shard_map/expert_rows/pallas_call | solution.py:135
  243.9 126.5 %all_to_all.11 = bf16[128,8,5120]{2,1,0:T(8,128)(2,1)S(1)} all-to-all(bf16[128,8,5120]{2,1,0:T(8,128)(2,1)} %bitcast.63), channel_id=1, replica_groups=mesh['dp'=16,'tensor'=8] {'dp','tensor'}, dimensions={0} | all-to-all | bytes 20971520 | tf_op jit(solution)/shard_map/all_to_all | solution.py:267
  370.4 6.5 %combine_rows.1 = bf16[128,4096]{1,0:T(8,128)(2,1)} custom-call(bf16[256,1024]{1,0:T(8,128)(2,1)S(1)} %fusion.16.main_w_ref, bf16[256,256]{1,0:T(8,128)(2,1)S(1)} %fusion.18.spill_w_ref, bf16[1024,5120]{1,0:T(8,128)(2,1)S(1)} %bitcast.49, bf16[1024,5120]{1,0:T(8,128)(2,1)S(1)} %bitcast.50, f32[128,4096]{1,0:T(8,128)S(1)} %get-tuple-element.36.hidden_ref), custom_call_target="tpu_custom_call" | custom-call | flops 4000000000 | bytes 15000000 | tf_op jit(solution)/shard_map/combine_rows/pallas_call | solution.py:181
  (46 shorter events, 0.6 us)
Async XLA Ops:
  1.3 5.4 %copy-start.3 = (bf16[1024,512]{1,0:T(8,128)(2,1)S(1)}, bf16[1024,512]{1,0:T(8,128)(2,1)}, u32[]{:S(2)}) copy-start(bf16[1024,512]{1,0:T(8,128)(2,1)} %param.9) | copy-start | bytes 3145732
  7.6 10.7 %copy-start.5 = (s32[128,8]{0,1:T(8,128)S(1)}, s32[128,8]{0,1:T(8,128)}, u32[]{:S(2)}) copy-start(s32[128,8]{0,1:T(8,128)} %param.13) | copy-start | bytes 12292
  7.6 11.0 %copy-start.6 = (f32[128,8]{0,1:T(8,128)S(1)}, f32[128,8]{0,1:T(8,128)}, u32[]{:S(2)}) copy-start(f32[128,8]{0,1:T(8,128)} %param.14) | copy-start | bytes 12292
  7.6 17.6 %collective-permute-start.1 = (bf16[256,1280]{1,0:T(8,128)(2,1)}, bf16[256,1280]{1,0:T(8,128)(2,1)S(1)}, u32[]{:S(2)}, u32[]{:S(2)}) collective-permute-start(bf16[256,1280]{1,0:T(8,128)(2,1)} %convolution_convert_fusion.4), channel_id=1, source_target_pairs={{0,2},{1,3},{2,4},{3,5},{4,6},{5,7},{6,0},{7,1},{8,10},{9,11},{10,... | collective-permute-start | bytes 1966088 | tf_op jit(solution)/shard_map/ppermute | solution.py:211
  9.6 15.6 %collective-permute-start.2 = (bf16[256,1280]{1,0:T(8,128)(2,1)}, bf16[256,1280]{1,0:T(8,128)(2,1)}, u32[]{:S(2)}, u32[]{:S(2)}) collective-permute-start(bf16[256,1280]{1,0:T(8,128)(2,1)} %convolution_convert_fusion.3), channel_id=1, source_target_pairs={{0,6},{1,7},{2,0},{3,1},{4,2},{5,3},{6,4},{7,5},{8,14},{9,15},{10,... | collective-permute-start | bytes 1966088 | tf_op jit(solution)/shard_map/ppermute | solution.py:211
  14.5 37.6 %collective-permute-start = (bf16[512,1536]{1,0:T(8,128)(2,1)}, bf16[512,1536]{1,0:T(8,128)(2,1)}, u32[]{:S(2)}, u32[]{:S(2)}) collective-permute-start(bf16[512,1536]{1,0:T(8,128)(2,1)} %convolution_convert_fusion.1), channel_id=1, source_target_pairs={{0,1},{1,0},{2,3},{3,2},{4,5},{5,4},{6,7},{7,6},{8,9},{9,8},{10,11... | collective-permute-start | bytes 4718600 | tf_op jit(solution)/shard_map/ppermute | solution.py:214
  19.8 3.0 copy-start.2
  26.8 31.5 %collective-permute-start.4 = (bf16[256,2560]{1,0:T(8,128)(2,1)S(1)}, bf16[256,2560]{1,0:T(8,128)(2,1)S(1)}, u32[]{:S(2)}, u32[]{:S(2)}) collective-permute-start(bf16[256,2560]{1,0:T(8,128)(2,1)S(1)} %pad_maximum_fusion.1), channel_id=1, source_target_pairs={{0,6},{1,7},{2,0},{3,1},{4,2},{5,3},{6,4},{7,5},{8,14},{9,15},{10,... | collective-permute-start | bytes 3932168 | tf_op jit(solution)/shard_map/ppermute | solution.py:211
  29.4 22.7 %copy-start.4 = (bf16[4,1,128,512]{3,2,1,0:T(8,128)(2,1)S(1)}, bf16[4,1,128,512]{3,2,1,0:T(8,128)(2,1)}, u32[]{:S(2)}) copy-start(bf16[4,1,128,512]{3,2,1,0:T(8,128)(2,1)} %get-tuple-element.46) | copy-start | bytes 1572868
  29.5 29.3 %collective-permute-start.3 = (bf16[256,2560]{1,0:T(8,128)(2,1)S(1)}, bf16[256,2560]{1,0:T(8,128)(2,1)S(1)}, u32[]{:S(2)}, u32[]{:S(2)}) collective-permute-start(bf16[256,2560]{1,0:T(8,128)(2,1)S(1)} %pad_maximum_fusion), channel_id=1, source_target_pairs={{0,2},{1,3},{2,4},{3,5},{4,6},{5,7},{6,0},{7,1},{8,10},{9,11},{10,... | collective-permute-start | bytes 3932168 | tf_op jit(solution)/shard_map/ppermute | solution.py:211
  54.6 13.0 %collective-permute-start.6 = (bf16[128,1536]{1,0:T(8,128)(2,1)S(1)}, bf16[128,1536]{1,0:T(8,128)(2,1)S(1)}, u32[]{:S(2)}, u32[]{:S(2)}) collective-permute-start(bf16[128,1536]{1,0:T(8,128)(2,1)S(1)} %get-tuple-element.39), channel_id=1, source_target_pairs={{0,2},{1,3},{2,4},{3,5},{4,6},{5,7},{6,0},{7,1},{8,10},{9,11},{10,... | collective-permute-start | bytes 1179656 | tf_op jit(solution)/shard_map/ppermute | solution.py:211
  54.7 20.6 %collective-permute-start.8 = (bf16[128,1536]{1,0:T(8,128)(2,1)S(1)}, bf16[128,1536]{1,0:T(8,128)(2,1)S(1)}, u32[]{:S(2)}, u32[]{:S(2)}) collective-permute-start(bf16[128,1536]{1,0:T(8,128)(2,1)S(1)} %get-tuple-element.40), channel_id=1, source_target_pairs={{0,4},{1,5},{2,6},{3,7},{4,0},{5,1},{6,2},{7,3},{8,12},{9,13},{10,... | collective-permute-start | bytes 1179656 | tf_op jit(solution)/shard_map/ppermute | solution.py:211
  57.1 18.2 %collective-permute-start.7 = (bf16[128,1536]{1,0:T(8,128)(2,1)S(1)}, bf16[128,1536]{1,0:T(8,128)(2,1)S(1)}, u32[]{:S(2)}, u32[]{:S(2)}) collective-permute-start(bf16[128,1536]{1,0:T(8,128)(2,1)S(1)} %get-tuple-element.41), channel_id=1, source_target_pairs={{0,6},{1,7},{2,0},{3,1},{4,2},{5,3},{6,4},{7,5},{8,14},{9,15},{10,... | collective-permute-start | bytes 1179656 | tf_op jit(solution)/shard_map/ppermute | solution.py:211
  59.7 15.8 %collective-permute-start.5 = (bf16[128,2560]{1,0:T(8,128)(2,1)S(1)}, bf16[128,2560]{1,0:T(8,128)(2,1)S(1)}, u32[]{:S(2)}, u32[]{:S(2)}) collective-permute-start(bf16[128,2560]{1,0:T(8,128)(2,1)S(1)} %fusion.15), channel_id=1, source_target_pairs={{0,1},{1,0},{2,3},{3,2},{4,5},{5,4},{6,7},{7,6},{8,9},{9,8},{10,11... | collective-permute-start | bytes 1966088 | tf_op jit(solution)/shard_map/ppermute | solution.py:214
  64.1 11.6 %copy-start = (bf16[128,4096]{1,0:T(8,128)(2,1)S(1)}, bf16[128,4096]{1,0:T(8,128)(2,1)}, u32[]{:S(2)}) copy-start(bf16[128,4096]{1,0:T(8,128)(2,1)} %residual_ref.1) | copy-start | bytes 3145732
  64.1 11.6 %copy-start.1 = (f32[4096]{0:T(1024)S(1)}, f32[4096]{0:T(1024)}, u32[]{:S(2)}) copy-start(f32[4096]{0:T(1024)} %param.12) | copy-start | bytes 49156
  75.7 139.3 %slice-start = ((s8[6291456]{0:T(1024)(128)(4,1)}), s8[4194304]{0:T(1024)(128)(4,1)S(1)}, s32[]{:S(2)}) async-start(s8[6291456]{0:T(1024)(128)(4,1)} %bitcast.52), calls=%async_computation.2 | async-start | bytes 8388608
  75.7 139.3 %slice-start.2 = ((s8[6291456]{0:T(1024)(128)(4,1)}), s8[2097152]{0:T(1024)(128)(4,1)S(1)}, s32[]{:S(2)}) async-start(s8[6291456]{0:T(1024)(128)(4,1)} %bitcast.55), calls=%async_computation.4 | async-start | bytes 4194304
  75.8 139.3 %slice-start.4 = ((s8[6291456]{0:T(1024)(128)(4,1)}), s8[4194304]{0:T(1024)(128)(4,1)S(1)}, s32[]{:S(2)}) async-start(s8[6291456]{0:T(1024)(128)(4,1)} %bitcast.58), calls=%async_computation.6 | async-start | bytes 8388608
  81.5 133.5 %slice-start.1 = ((s8[6291456]{0:T(1024)(128)(4,1)}), s8[2097152]{0:T(1024)(128)(4,1)S(1)}, s32[]{:S(2)}) async-start(s8[6291456]{0:T(1024)(128)(4,1)} %bitcast.52), calls=%async_computation.3 | async-start | bytes 4194304
  81.5 133.5 %slice-start.3 = ((s8[6291456]{0:T(1024)(128)(4,1)}), s8[4194304]{0:T(1024)(128)(4,1)S(1)}, s32[]{:S(2)}) async-start(s8[6291456]{0:T(1024)(128)(4,1)} %bitcast.55), calls=%async_computation.5 | async-start | bytes 8388608
  81.5 133.5 %slice-start.5 = ((s8[6291456]{0:T(1024)(128)(4,1)}), s8[2097152]{0:T(1024)(128)(4,1)S(1)}, s32[]{:S(2)}) async-start(s8[6291456]{0:T(1024)(128)(4,1)} %bitcast.58), calls=%async_computation.7 | async-start | bytes 4194304

commit v6 on v5

--- a/solution.py
+++ b/solution.py
@@ -202,7 +202,7 @@
 
 def project_scatter(attn_heads, out_weight, toks):
     width = out_weight.shape[1]
-    first = width * 5 // 8
+    first = width * 9 // 16
     at = lax.axis_index("tensor")
     x, z = at // 2, at % 2
     heads = attn_heads.reshape(4, 2, toks, attn_heads.shape[1])

time: 377 us -> 383 us (1.016)
  blocking collectives: 260 us -> 255 us
  waiting for transfers between devices: 35.6 us -> 40 us
    all_to_all x2, blocking collectives: 260 us -> 255 us  [swap(): lax.all_to_all(v.reshape(experts, MAIN, cols), ('dp', 'tensor'), split_ax...]
  transfers between devices with their start and end apart: 9 -> 9, of which waited for: 5 -> 5; matrix products, arithmetic and copies ran while one was open for 4% -> 5% of each run, Pallas kernels for 0% -> 0%
where the time goes in v6:
time: 383 us; the launch traced here: 382 us
  blocking collectives  255 us (67%)
  Pallas kernels  41 us (11%)
  waiting for transfers between devices  40 us (10%)
  matrix products  18.1 us (5%)
  starting transfers between devices  16.3 us (4%)
  other arithmetic  5.88 us (2%)
  local copies, waits for them, and re-layouts  5.15 us (1%)
    all_to_all x2, blocking collectives, swap(): lax.all_to_all(v.reshape(experts, MAIN, cols), ('dp', 'tensor'), split_ax...  255 us
    pallas_call x1, Pallas kernels, expert(): pl.pallas_call(kernel, grid=(flat // block,), in_specs=[pl.BlockSpec((blo...  28.8 us
    ppermute x2, waiting for transfers between devices, along_z(): return lax.ppermute(v, 'tensor', [(i, i ^ 1) for i in range(8)])  25.2 us
    dot_general x8, matrix products, dot(): return jnp.dot(a, b, preferred_element_type=F32)  18.1 us
    ppermute x7, waiting for transfers between devices, along_x(): lax.ppermute(v, 'tensor', [(i * 2 + j, (i + by) % 4 * 2 + j) for i in ran...  14.8 us
    ppermute x7, starting transfers between devices, along_x(): lax.ppermute(v, 'tensor', [(i * 2 + j, (i + by) % 4 * 2 + j) for i in ran...  9.64 us
  transfers between devices with their start and end apart: 9, of which 5 were waited for; matrix products, arithmetic and copies ran while one was open for 5% of the time, Pallas kernels for 0%

profile of v6, /device:TPU:1, one launch (start us, length us, event | category | flops | bytes accessed | tf_op | source)
XLA Modules:
  0.0 382.3 jit_solution(2186016819674086673)
XLA Ops:
  0.0 2.1 constant_dynamic-slice_fusion.2
  2.1 2.7 convolution_convert_fusion.3
  4.8 2.6 convolution_convert_fusion.4
  7.4 0.9 constant_dynamic-slice_fusion.5
  8.3 2.0 collective-permute-start.1
  10.3 1.3 collective-permute-start.2
  11.7 3.8 %convolution_convert_fusion.1 = bf16[512,1792]{1,0:T(8,128)(2,1)} fusion(bf16[512,512]{1,0:T(8,128)(2,1)S(1)} %bitcast.75, bf16[512,4096]{1,0:T(8,128)(2,1)} %param.10), kind=kOutput, calls=%fused_computation.3 | convolution fusion | flops 940441600 | bytes 4194304 | tf_op jit(solution)/shard_map/dot_general | solution.py:16
  15.5 3.7 collective-permute-start
  19.2 0.1 fusion.17
  19.3 0.1 fusion.12.slot_ref
  19.6 0.8 fusion.3
  20.4 0.1 eq.75
  20.6 0.7 copy.18
  21.4 0.1 broadcast_bitcast_fusion
  21.4 2.5 fusion.1
  24.0 0.5 collective-permute-done.1
  24.5 0.1 slice.59
  24.6 1.2 add_convert_fusion.1
  25.8 1.1 pad_maximum_fusion.1
  27.0 2.6 collective-permute-start.4
  29.6 1.2 add_convert_fusion.2
  30.8 1.1 pad_maximum_fusion
  31.9 0.6 broadcast_compare_fusion.1
  32.5 0.1 eq.69
  32.6 0.1 broadcast_in_dim.64
  32.8 0.1 copy.19
  32.9 0.2 copy.17
  33.1 0.2 copy.16
  33.3 0.1 broadcast_compare_fusion
  33.4 25.2 %collective-permute-done = bf16[512,1792]{1,0:T(8,128)(2,1)} collective-permute-done((bf16[512,1792]{1,0:T(8,128)(2,1)}, bf16[512,1792]{1,0:T(8,128)(2,1)}, u32[]{:S(2)}, u32[]{:S(2)}) %collective-permute-start) | collective-permute-done | bytes 1835040 | tf_op jit(solution)/shard_map/ppermute | solution.py:214
  58.6 3.5 add_convert_fusion
  62.1 0.1 dynamic-slice_bitcast_fusion.2
  62.2 0.1 collective-permute-start.6
  62.3 2.4 collective-permute-start.8
  64.8 1.2 collective-permute-start.7
  65.9 2.1 convert_add_fusion
  68.0 0.1 fusion.15
  68.1 2.9 collective-permute-start.5
  71.1 2.8 collective-permute-done.6
  73.9 9.4 %collective-permute-done.8 = bf16[128,1792]{1,0:T(8,128)(2,1)S(1)} collective-permute-done((bf16[128,1792]{1,0:T(8,128)(2,1)S(1)}, bf16[128,1792]{1,0:T(8,128)(2,1)S(1)}, u32[]{:S(2)}, u32[]{:S(2)}) %collective-permute-start.8) | collective-permute-done | bytes 458784 | tf_op jit(solution)/shard_map/ppermute | solution.py:211
  83.3 2.0 collective-permute-done.7
  85.3 0.2 fusion.14.far_ref
  85.6 0.1 bitcast_add_fusion.near_ref
  85.8 5.7 %build_rows.1 = (bf16[1024,5120]{1,0:T(8,128)(2,1)S(1)}, f32[128,4096]{1,0:T(8,128)S(1)}) custom-call(s32[128,128]{1,0:T(8,128)S(1)} %fusion.12.slot_ref, f32[128,2304]{1,0:T(8,128)S(1)} %bitcast_add_fusion.near_ref, f32[128,1792]{1,0:T(8,128)S(1)} %fusion.14.far_ref, bf16[128,4096]{1,0:T(8,128)(2,1)S(1)} %copy-done, f32[1,4096]{1,0:T(1,128)S(1)} %bitcast.61), custom_call_target="tpu_custom_call" | custom-call | flops 3000000000 | bytes 15000000 | tf_op jit(solution)/shard_map/build_rows/pallas_call | solution.py:82
  91.5 128.9 %all_to_all.10 = bf16[128,8,5120]{2,1,0:T(8,128)(2,1)} all-to-all(bf16[128,8,5120]{2,1,0:T(8,128)(2,1)S(1)} %bitcast.51), channel_id=1, replica_groups=mesh['dp'=16,'tensor'=8] {'dp','tensor'}, dimensions={0} | all-to-all | bytes 20971520 | tf_op jit(solution)/shard_map/all_to_all | solution.py:267
  220.5 28.8 %expert_rows.1 = bf16[1024,5120]{1,0:T(8,128)(2,1)} custom-call(bf16[1024,5120]{1,0:T(8,128)(2,1)} %bitcast.62, bf16[4096,768]{1,0:T(8,128)(2,1)S(1)} %bitcast.54, bf16[4096,768]{1,0:T(8,128)(2,1)S(1)} %bitcast.57, bf16[768,4096]{1,0:T(8,128)(2,1)S(1)} %bitcast.60), custom_call_target="tpu_custom_call" | custom-call | flops 24000000000 | bytes 40000000 | tf_op jit(solution)/shard_map/expert_rows/pallas_call | solution.py:135
  249.3 126.5 %all_to_all.11 = bf16[128,8,5120]{2,1,0:T(8,128)(2,1)S(1)} all-to-all(bf16[128,8,5120]{2,1,0:T(8,128)(2,1)} %bitcast.63), channel_id=1, replica_groups=mesh['dp'=16,'tensor'=8] {'dp','tensor'}, dimensions={0} | all-to-all | bytes 20971520 | tf_op jit(solution)/shard_map/all_to_all | solution.py:267
  375.8 6.5 %combine_rows.1 = bf16[128,4096]{1,0:T(8,128)(2,1)} custom-call(bf16[256,1024]{1,0:T(8,128)(2,1)S(1)} %fusion.16.main_w_ref, bf16[256,256]{1,0:T(8,128)(2,1)S(1)} %fusion.18.spill_w_ref, bf16[1024,5120]{1,0:T(8,128)(2,1)S(1)} %bitcast.49, bf16[1024,5120]{1,0:T(8,128)(2,1)S(1)} %bitcast.50, f32[128,4096]{1,0:T(8,128)S(1)} %get-tuple-element.36.hidden_ref), custom_call_target="tpu_custom_call" | custom-call | flops 4000000000 | bytes 15000000 | tf_op jit(solution)/shard_map/combine_rows/pallas_call | solution.py:181
  (52 shorter events, 0.5 us)
Async XLA Ops:
  2.1 5.3 %copy-start.4 = (bf16[1024,512]{1,0:T(8,128)(2,1)S(1)}, bf16[1024,512]{1,0:T(8,128)(2,1)}, u32[]{:S(2)}) copy-start(bf16[1024,512]{1,0:T(8,128)(2,1)} %param.9) | copy-start | bytes 3145732
  8.3 10.9 %copy-start.8 = (s32[128,8]{0,1:T(8,128)S(1)}, s32[128,8]{0,1:T(8,128)}, u32[]{:S(2)}) copy-start(s32[128,8]{0,1:T(8,128)} %param.13) | copy-start | bytes 12292
  8.3 11.2 %copy-start.9 = (f32[128,8]{0,1:T(8,128)S(1)}, f32[128,8]{0,1:T(8,128)}, u32[]{:S(2)}) copy-start(f32[128,8]{0,1:T(8,128)} %param.14) | copy-start | bytes 12292
  8.3 11.3 %copy-start.2 = (bf16[512,4096]{1,0:T(8,128)(2,1)S(1)}, bf16[512,4096]{1,0:T(8,128)(2,1)}, u32[]{:S(2)}) copy-start(bf16[512,4096]{1,0:T(8,128)(2,1)} %param.10) | copy-start | bytes 12582916
  8.3 16.2 %collective-permute-start.1 = (bf16[256,1152]{1,0:T(8,128)(2,1)}, bf16[256,1152]{1,0:T(8,128)(2,1)}, u32[]{:S(2)}, u32[]{:S(2)}) collective-permute-start(bf16[256,1152]{1,0:T(8,128)(2,1)} %convolution_convert_fusion.4), channel_id=1, source_target_pairs={{0,2},{1,3},{2,4},{3,5},{4,6},{5,7},{6,0},{7,1},{8,10},{9,11},{10,... | collective-permute-start | bytes 1769480 | tf_op jit(solution)/shard_map/ppermute | solution.py:211
  10.3 14.2 %collective-permute-start.2 = (bf16[256,1152]{1,0:T(8,128)(2,1)}, bf16[256,1152]{1,0:T(8,128)(2,1)}, u32[]{:S(2)}, u32[]{:S(2)}) collective-permute-start(bf16[256,1152]{1,0:T(8,128)(2,1)} %convolution_convert_fusion.3), channel_id=1, source_target_pairs={{0,6},{1,7},{2,0},{3,1},{4,2},{5,3},{6,4},{7,5},{8,14},{9,15},{10,... | collective-permute-start | bytes 1769480 | tf_op jit(solution)/shard_map/ppermute | solution.py:211
  15.5 43.1 %collective-permute-start = (bf16[512,1792]{1,0:T(8,128)(2,1)}, bf16[512,1792]{1,0:T(8,128)(2,1)}, u32[]{:S(2)}, u32[]{:S(2)}) collective-permute-start(bf16[512,1792]{1,0:T(8,128)(2,1)} %convolution_convert_fusion.1), channel_id=1, source_target_pairs={{0,1},{1,0},{2,3},{3,2},{4,5},{5,4},{6,7},{7,6},{8,9},{9,8},{10,11... | collective-permute-start | bytes 5505032 | tf_op jit(solution)/shard_map/ppermute | solution.py:214
  27.0 4.9 %copy-start.6 = (s32[256,128]{0,1:T(8,128)S(1)}, s32[256,128]{0,1:T(8,128)}, u32[]{:S(2)}) copy-start(s32[256,128]{0,1:T(8,128)} %copy.18) | copy-start | bytes 393220
  27.0 38.9 %collective-permute-start.4 = (bf16[256,2304]{1,0:T(8,128)(2,1)}, bf16[256,2304]{1,0:T(8,128)(2,1)}, u32[]{:S(2)}, u32[]{:S(2)}) collective-permute-start(bf16[256,2304]{1,0:T(8,128)(2,1)} %pad_maximum_fusion.1), channel_id=1, source_target_pairs={{0,6},{1,7},{2,0},{3,1},{4,2},{5,3},{6,4},{7,5},{8,14},{9,15},{10,... | collective-permute-start | bytes 3538952 | tf_op jit(solution)/shard_map/ppermute | solution.py:211
  31.9 34.1 %collective-permute-start.3 = (bf16[256,2304]{1,0:T(8,128)(2,1)}, bf16[256,2304]{1,0:T(8,128)(2,1)S(1)}, u32[]{:S(2)}, u32[]{:S(2)}) collective-permute-start(bf16[256,2304]{1,0:T(8,128)(2,1)} %pad_maximum_fusion), channel_id=1, source_target_pairs={{0,2},{1,3},{2,4},{3,5},{4,6},{5,7},{6,0},{7,1},{8,10},{9,11},{10,... | collective-permute-start | bytes 3538952 | tf_op jit(solution)/shard_map/ppermute | solution.py:211
  58.6 7.3 %copy-start.3 = (bf16[512,4096]{1,0:T(8,128)(2,1)S(1)}, bf16[512,4096]{1,0:T(8,128)(2,1)}, u32[]{:S(2)}) copy-start(bf16[512,4096]{1,0:T(8,128)(2,1)} %param.10) | copy-start | bytes 12582916
  62.1 3.8 copy-start.5
  62.2 11.6 %collective-permute-start.6 = (bf16[128,1792]{1,0:T(8,128)(2,1)S(1)}, bf16[128,1792]{1,0:T(8,128)(2,1)S(1)}, u32[]{:S(2)}, u32[]{:S(2)}) collective-permute-start(bf16[128,1792]{1,0:T(8,128)(2,1)S(1)} %get-tuple-element.39), channel_id=1, source_target_pairs={{0,2},{1,3},{2,4},{3,5},{4,6},{5,7},{6,0},{7,1},{8,10},{9,11},{10,... | collective-permute-start | bytes 1376264 | tf_op jit(solution)/shard_map/ppermute | solution.py:211
  62.3 21.0 %collective-permute-start.8 = (bf16[128,1792]{1,0:T(8,128)(2,1)S(1)}, bf16[128,1792]{1,0:T(8,128)(2,1)S(1)}, u32[]{:S(2)}, u32[]{:S(2)}) collective-permute-start(bf16[128,1792]{1,0:T(8,128)(2,1)S(1)} %get-tuple-element.40), channel_id=1, source_target_pairs={{0,4},{1,5},{2,6},{3,7},{4,0},{5,1},{6,2},{7,3},{8,12},{9,13},{10,... | collective-permute-start | bytes 1376264 | tf_op jit(solution)/shard_map/ppermute | solution.py:211
  64.8 6.3 %copy-start.7 = (pred[256,128]{0,1:T(8,128)(4,1)S(1)}, pred[256,128]{0,1:T(8,128)(4,1)}, u32[]{:S(2)}) copy-start(pred[256,128]{0,1:T(8,128)(4,1)} %broadcast_compare_fusion.1) | copy-start | bytes 98308
  64.8 20.6 %collective-permute-start.7 = (bf16[128,1792]{1,0:T(8,128)(2,1)S(1)}, bf16[128,1792]{1,0:T(8,128)(2,1)S(1)}, u32[]{:S(2)}, u32[]{:S(2)}) collective-permute-start(bf16[128,1792]{1,0:T(8,128)(2,1)S(1)} %get-tuple-element.41), channel_id=1, source_target_pairs={{0,6},{1,7},{2,0},{3,1},{4,2},{5,3},{6,4},{7,5},{8,14},{9,15},{10,... | collective-permute-start | bytes 1376264 | tf_op jit(solution)/shard_map/ppermute | solution.py:211
  68.1 17.5 %collective-permute-start.5 = (bf16[128,2304]{1,0:T(8,128)(2,1)S(1)}, bf16[128,2304]{1,0:T(8,128)(2,1)S(1)}, u32[]{:S(2)}, u32[]{:S(2)}) collective-permute-start(bf16[128,2304]{1,0:T(8,128)(2,1)S(1)} %fusion.15), channel_id=1, source_target_pairs={{0,1},{1,0},{2,3},{3,2},{4,5},{5,4},{6,7},{7,6},{8,9},{9,8},{10,11... | collective-permute-start | bytes 1769480 | tf_op jit(solution)/shard_map/ppermute | solution.py:214
  71.1 14.6 %copy-start = (bf16[128,4096]{1,0:T(8,128)(2,1)S(1)}, bf16[128,4096]{1,0:T(8,128)(2,1)}, u32[]{:S(2)}) copy-start(bf16[128,4096]{1,0:T(8,128)(2,1)} %residual_ref.1) | copy-start | bytes 3145732
  71.1 14.6 %copy-start.1 = (f32[4096]{0:T(1024)S(1)}, f32[4096]{0:T(1024)}, u32[]{:S(2)}) copy-start(f32[4096]{0:T(1024)} %param.12) | copy-start | bytes 49156
  85.7 134.7 %slice-start = ((s8[6291456]{0:T(1024)(128)(4,1)}), s8[4194304]{0:T(1024)(128)(4,1)S(1)}, s32[]{:S(2)}) async-start(s8[6291456]{0:T(1024)(128)(4,1)} %bitcast.52), calls=%async_computation.2 | async-start | bytes 8388608
  85.7 134.7 %slice-start.2 = ((s8[6291456]{0:T(1024)(128)(4,1)}), s8[2097152]{0:T(1024)(128)(4,1)S(1)}, s32[]{:S(2)}) async-start(s8[6291456]{0:T(1024)(128)(4,1)} %bitcast.55), calls=%async_computation.4 | async-start | bytes 4194304
  85.7 134.7 %slice-start.4 = ((s8[6291456]{0:T(1024)(128)(4,1)}), s8[4194304]{0:T(1024)(128)(4,1)S(1)}, s32[]{:S(2)}) async-start(s8[6291456]{0:T(1024)(128)(4,1)} %bitcast.58), calls=%async_computation.6 | async-start | bytes 8388608
  91.5 129.0 %slice-start.1 = ((s8[6291456]{0:T(1024)(128)(4,1)}), s8[2097152]{0:T(1024)(128)(4,1)S(1)}, s32[]{:S(2)}) async-start(s8[6291456]{0:T(1024)(128)(4,1)} %bitcast.52), calls=%async_computation.3 | async-start | bytes 4194304
  91.5 129.0 %slice-start.3 = ((s8[6291456]{0:T(1024)(128)(4,1)}), s8[4194304]{0:T(1024)(128)(4,1)S(1)}, s32[]{:S(2)}) async-start(s8[6291456]{0:T(1024)(128)(4,1)} %bitcast.55), calls=%async_computation.5 | async-start | bytes 8388608
  91.5 129.0 %slice-start.5 = ((s8[6291456]{0:T(1024)(128)(4,1)}), s8[2097152]{0:T(1024)(128)(4,1)S(1)}, s32[]{:S(2)}) async-start(s8[6291456]{0:T(1024)(128)(4,1)} %bitcast.58), calls=%async_computation.7 | async-start | bytes 4194304
